TPU v7x, 512 devices: a whole 4x8x8 slice. The times are simulated.
512 devices in a mesh: sector: 64 (over y, z_hi, core), span: 8 (over x, z_lo).
Axes of the slice: x: 4, y: 8, z: 8 (z_hi: 4, z_lo: 2; z = z_hi * 2 + z_lo), core: 2. Of those that a mesh axis runs over, the one named last changes fastest.
Arguments:
- node_latents: bfloat16 [131072, 128], P(('sector', 'span')), may hold values from -6 to 6
- edge_latents: bfloat16 [524288, 128], P(('sector', 'span')), may hold values from -6 to 6
- senders: int32 [524288], P(('sector', 'span')), may hold values from 0 to 383
- receivers: int32 [524288], P(('sector', 'span')), may hold values from 0 to 255
- halo_rows: int32 [512, 4, 32], P(('sector', 'span')), may hold values from 0 to 255
- counts: int32 [512], P(('sector', 'span')), may hold values from 128 to 1024, as said below
- cotangent: bfloat16 [131072, 128], P(('sector', 'span')), may hold values from -8 to 8
- edge_first: bfloat16 [2, 384, 128], replicated, may hold values from -0.3125 to 0.3125
- edge_bias: float32 [2, 128], replicated, may hold values from -3 to 3
- edge_second: bfloat16 [2, 128, 128], replicated, may hold values from -0.5 to 0.5
- edge_gain: float32 [2, 128], replicated, may hold values from 2 to 4
- node_first: bfloat16 [2, 256, 128], replicated, may hold values from -0.375 to 0.375
- node_bias: float32 [2, 128], replicated, may hold values from -3 to 3
- node_second: bfloat16 [2, 128, 128], replicated, may hold values from -0.5 to 0.5
- node_gain: float32 [2, 128], replicated, may hold values from 2 to 4
Outputs:
- node_grad: bfloat16 [131072, 128], P(('sector', 'span'))
- edge_grad: bfloat16 [524288, 128], P(('sector', 'span'))
- edge_first_grad: float32 [2, 384, 128], replicated
- edge_bias_grad: float32 [2, 128], replicated
- edge_second_grad: float32 [2, 128, 128], replicated
- edge_gain_grad: float32 [2, 128], replicated
- node_first_grad: float32 [2, 256, 128], replicated
- node_bias_grad: float32 [2, 128], replicated
- node_second_grad: float32 [2, 128, 128], replicated
- node_gain_grad: float32 [2, 128], replicated
Inputs may be any that keep to these rules, and one draw needn't show every extreme that they name: `counts`: some tile uses all 1024 slots.
All inputs are finite; a program needn't handle non-finite values.
Results may differ from a plain program's by a relative error of at most 0.03.
Values may be sent and summed in bfloat16 or wider, within the bound.
A program may use at most 64 MiB of HBM per device.

v0:
```python
import jax
import jax.numpy as jnp
from jax import lax
from jax.sharding import PartitionSpec as P

STEPS = 2


EPS = 1e-05


def passed_along(array, axis, by):
    peers = lax.axis_size(axis)
    return lax.ppermute(array, axis, [(i, (i + by) % peers) for i in range(peers)])


def shifted(value, axis, steps):
    count = lax.axis_size(axis)
    leading, last = (max(0, -steps), min(count, count - steps))
    return lax.ppermute(value, axis, [(source, source + steps) for source in range(leading, last)])


def normalize(projected, gain):
    average = jnp.mean(projected, axis=-1, keepdims=True)
    centred = projected - average
    spread = jnp.mean(centred * centred, axis=-1, keepdims=True)
    return centred * lax.rsqrt(spread + EPS) * gain


def network(inputs, first, bias, second, gain):
    linear = jnp.dot(inputs, first.astype(jnp.bfloat16), preferred_element_type=jnp.float32) + bias
    activated = jax.nn.silu(linear).astype(jnp.bfloat16)
    projected = jnp.dot(activated, second.astype(jnp.bfloat16), preferred_element_type=jnp.float32)
    return normalize(projected, gain)


def tile_step(own_rows, halo_in, edge_rows, sender_ids, receiver_ids, live_mask, params):
    edge_first, edge_bias, edge_second, edge_gain, node_first, node_bias, node_second, node_gain = (
        params
    )
    extended = jnp.concatenate([own_rows, halo_in], axis=0).astype(jnp.bfloat16)
    own_half = own_rows.astype(jnp.bfloat16)
    edge_half = edge_rows.astype(jnp.bfloat16)
    edge_input = jnp.concatenate(
        [
            jnp.take(extended, sender_ids, axis=0),
            jnp.take(own_half, receiver_ids, axis=0),
            edge_half,
        ],
        axis=1,
    )
    update = network(edge_input, edge_first, edge_bias, edge_second, edge_gain)
    new_edge = (edge_rows + live_mask[:, None] * update).astype(jnp.bfloat16)
    new_edge_f = lax.optimization_barrier(new_edge).astype(jnp.float32)
    summed = jax.ops.segment_sum(
        live_mask[:, None] * new_edge_f, receiver_ids, num_segments=own_rows.shape[0]
    ).astype(jnp.bfloat16)
    node_input = jnp.concatenate([own_half, summed], axis=1)
    node_update = network(node_input, node_first, node_bias, node_second, node_gain)
    new_node = (own_rows + node_update).astype(jnp.bfloat16)
    return (new_node, new_edge_f)


def per_device(
    node_latents,
    edge_latents,
    senders,
    receivers,
    halo_rows,
    counts,
    cotangent,
    edge_first,
    edge_bias,
    edge_second,
    edge_gain,
    node_first,
    node_bias,
    node_second,
    node_gain,
):
    row_lists = halo_rows[0]
    halo_count = row_lists.shape[1]
    width = node_latents.shape[1]
    node_total = node_latents.shape[0]
    live_mask = (jnp.arange(edge_latents.shape[0], dtype=jnp.int32) < counts[0]).astype(jnp.float32)
    weights = (
        edge_first.astype(jnp.float32),
        edge_bias,
        edge_second.astype(jnp.float32),
        edge_gain,
        node_first.astype(jnp.float32),
        node_bias,
        node_second.astype(jnp.float32),
        node_gain,
    )

    def local_step(own_rows, halo_in, edge_rows, params):
        return tile_step(own_rows, halo_in, edge_rows, senders, receivers, live_mask, params)

    node_f = node_latents.astype(jnp.float32)
    edge_f = edge_latents.astype(jnp.float32)
    pullbacks = []
    for layer_index in range(STEPS):
        outgoing = node_f[row_lists].astype(jnp.bfloat16)
        from_lower = passed_along(outgoing[1], "sector", 1)
        from_upper = passed_along(outgoing[0], "sector", -1)
        from_below = shifted(outgoing[3], "span", 1)
        from_above = shifted(outgoing[2], "span", -1)
        received = jnp.concatenate([from_lower, from_upper, from_below, from_above], axis=0).astype(
            jnp.float32
        )
        layer_params = tuple((weight[layer_index] for weight in weights))
        (new_node, edge_f), pullback = jax.vjp(local_step, node_f, received, edge_f, layer_params)
        pullbacks.append(pullback)
        node_f = new_node.astype(jnp.float32)
    node_cot = cotangent
    edge_cot = jnp.zeros_like(edge_f)
    grad_parts = [None] * STEPS
    for layer_index in reversed(range(STEPS)):
        own_cot, halo_cot, edge_cot, param_cot = pullbacks[layer_index]((node_cot, edge_cot))
        pieces = halo_cot.reshape(4, halo_count, width)
        to_first = passed_along(pieces[1], "sector", 1)
        to_second = passed_along(pieces[0], "sector", -1)
        to_third = shifted(pieces[3], "span", 1)
        to_fourth = shifted(pieces[2], "span", -1)
        stacked = jnp.stack([to_first, to_second, to_third, to_fourth]).reshape(-1, width)
        combined = own_cot + jnp.zeros((node_total, width), jnp.float32).at[
            row_lists.reshape(-1)
        ].add(stacked)
        node_cot = combined.astype(jnp.bfloat16)
        grad_parts[layer_index] = param_cot
    stacked_grads = tuple(
        (
            jnp.stack([grad_parts[layer_index][member] for layer_index in range(STEPS)])
            for member in range(8)
        )
    )
    stacked_grads = lax.psum(stacked_grads, ("sector", "span"))
    scale = jnp.float32(node_total * lax.axis_size("sector") * lax.axis_size("span")) ** (-0.5)
    scaled = tuple((grad * scale for grad in stacked_grads))
    edge_grad = edge_cot.astype(jnp.bfloat16)
    return (
        node_cot,
        edge_grad,
        scaled[0],
        scaled[1],
        scaled[2],
        scaled[3],
        scaled[4],
        scaled[5],
        scaled[6],
        scaled[7],
    )


def solution(mesh):
    placed = (
        P(("sector", "span"), None),
        P(("sector", "span"), None),
        P(("sector", "span")),
        P(("sector", "span")),
        P(("sector", "span"), None, None),
        P(("sector", "span")),
        P(("sector", "span"), None),
        P(),
        P(),
        P(),
        P(),
        P(),
        P(),
        P(),
        P(),
    )
    return jax.shard_map(
        per_device,
        mesh=mesh,
        in_specs=placed,
        out_specs=(
            P(("sector", "span"), None),
            P(("sector", "span"), None),
            P(),
            P(),
            P(),
            P(),
            P(),
            P(),
            P(),
            P(),
        ),
        check_vma=False,
    )
```

profile of v0, /device:TPU:1, one launch (start us, length us, event | category | flops | bytes accessed | tf_op | source)
XLA Modules:
  0.0 559.5 jit_solution(14825808094811139536)
XLA Ops:
  9.1 1.3 compare_select_fusion
  12.4 8.8 %collective-permute-start.1 = (bf16[32,128]{1,0:T(8,128)(2,1)S(1)}, bf16[32,128]{1,0:T(8,128)(2,1)S(1)}, u32[]{:S(2)}, u32[]{:S(2)}) collective-permute-start(bf16[32,128]{1,0:T(8,128)(2,1)S(1)} %get-tuple-element.95), channel_id=1, source_target_pairs={{0,504},{8,0},{16,8},{24,16},{32,24},{40,32},{48,40},{56,48},{64,5... | collective-permute-start | bytes 24584 | tf_op jit(solution)/shard_map/ppermute | solution.py:14
  21.2 1.9 collective-permute-start
  23.1 4.3 collective-permute-start.2
  36.7 3.2 gather_fusion.5
  41.1 3.2 gather_fusion.4
  47.1 6.2 %scatter_custom_fusion = f32[256,128]{1,0:T(8,128)S(1)} fusion(s32[1024]{0:T(1024)} %param.22, f32[1024,128]{1,0:T(8,128)S(1)} %copy.82, f32[]{:T(128)} %constant.48.clone.1), kind=kCustom, calls=%fused_computation.168 | custom fusion | flops 131072 | bytes 131584 | tf_op jit(solution)/shard_map/jvp()/scatter-add | solution.py:55
  55.2 1.3 collective-permute-start.7
  56.5 7.9 %collective-permute-start.5 = (bf16[32,128]{0,1:T(8,128)(2,1)S(1)}, bf16[32,128]{0,1:T(8,128)(2,1)S(1)}, u32[]{:S(2)}, u32[]{:S(2)}) collective-permute-start(bf16[32,128]{0,1:T(8,128)(2,1)S(1)} %get-tuple-element.91), channel_id=1, source_target_pairs={{0,504},{8,0},{16,8},{24,16},{32,24},{40,32},{48,40},{56,48},{64,5... | collective-permute-start | bytes 24584 | tf_op jit(solution)/shard_map/ppermute | solution.py:14
  64.4 1.9 collective-permute-start.4
  66.4 4.6 collective-permute-start.6
  71.0 3.2 gather_fusion.7
  74.7 3.2 gather_fusion.6
  81.3 6.4 %scatter_custom_fusion.1 = f32[256,128]{1,0:T(8,128)S(1)} fusion(s32[1024]{0:T(1024)} %param.22, f32[1024,128]{1,0:T(8,128)S(1)} %copy.89, f32[]{:T(128)} %constant.48.clone.1), kind=kCustom, calls=%fused_computation.166 | custom fusion | flops 131072 | bytes 131584 | tf_op jit(solution)/shard_map/jvp()/scatter-add | solution.py:55
  91.0 2.8 gather_fusion.2
  99.8 6.2 %scatter_custom_fusion.3 = bf16[384,128]{1,0:T(8,128)(2,1)S(1)} fusion(s32[1024]{0:T(1024)} %get-tuple-element.104, bf16[1024,128]{1,0:T(8,128)(2,1)S(1)} %copy.95, bf16[]{:T(256)} %constant.75.clone.1), kind=kCustom, calls=%fused_computation.176 | custom fusion | flops 131072 | bytes 98816 | tf_op jit(solution)/shard_map/transpose(jvp(jit(_take)))/scatter-add | solution.py:46
  107.1 6.1 %scatter_fusion = bf16[256,128]{1,0:T(8,128)(2,1)S(1)} fusion(bf16[256,128]{1,0:T(8,128)(2,1)S(1)} %get-tuple-element.80, s32[1024]{0:T(1024)S(1)} %copy-done.29, bf16[1024,128]{1,0:T(8,128)(2,1)S(1)} %copy.93), kind=kCustom, calls=%fused_computation.10 | custom fusion | flops 131072 | bytes 790528 | tf_op jit(solution)/shard_map/transpose(jvp(jit(_take)))/scatter-add | solution.py:47
  113.4 1.9 collective-permute-start.8
  115.3 7.9 %collective-permute-start.9 = (f32[32,128]{0,1:T(8,128)}, f32[32,128]{0,1:T(8,128)S(1)}, u32[]{:S(2)}, u32[]{:S(2)}) collective-permute-start(f32[32,128]{0,1:T(8,128)} %get-tuple-element.87), channel_id=1, source_target_pairs={{0,504},{8,0},{16,8},{24,16},{32,24},{40,32},{48,40},{56,48},{64,5... | collective-permute-start | bytes 49160 | tf_op jit(solution)/shard_map/ppermute | solution.py:14
  123.2 4.3 collective-permute-start.10
  129.9 3.1 collective-permute-done.11
  133.2 1.5 scatter_fusion.1
  138.5 2.8 gather_fusion.3
  147.1 6.2 %scatter_custom_fusion.6 = bf16[384,128]{1,0:T(8,128)(2,1)S(1)} fusion(s32[1024]{0:T(1024)} %get-tuple-element.104, bf16[1024,128]{1,0:T(8,128)(2,1)S(1)} %copy.107, bf16[]{:T(256)} %constant.75.clone.1), kind=kCustom, calls=%fused_computation.174 | custom fusion | flops 131072 | bytes 98816 | tf_op jit(solution)/shard_map/transpose(jvp(jit(_take)))/scatter-add | solution.py:46
  153.7 102.2 %all-reduce = (f32[2,128]{1,0:T(2,128)S(1)}, f32[2,128]{1,0:T(2,128)S(1)}, f32[2,128]{1,0:T(2,128)S(1)}, f32[2,128]{1,0:T(2,128)S(1)}) all-reduce(f32[2,128]{1,0:T(2,128)S(1)} %pad_maximum_fusion.14, f32[2,128]{1,0:T(2,128)S(1)} %pad_maximum_fusion.15, ...), channel_id=1, replica_groups=mesh['sector'=64,'span'=8] {'sector','span'}, use_global_device_ids=true, to_apply=%region_27.30 | all-reduce | flops 1024 | bytes 8192 | tf_op jit(solution)/shard_map/psum | solution.py:138
  257.3 6.1 %scatter_fusion.2 = bf16[256,128]{1,0:T(8,128)(2,1)S(1)} fusion(bf16[256,128]{1,0:T(8,128)(2,1)S(1)} %get-tuple-element.78, s32[1024]{0:T(1024)S(1)} %copy-done.29, bf16[1024,128]{1,0:T(8,128)(2,1)S(1)} %copy.105), kind=kCustom, calls=%fused_computation.13 | custom fusion | flops 131072 | bytes 790528 | tf_op jit(solution)/shard_map/transpose(jvp(jit(_take)))/scatter-add | solution.py:47
  263.6 2.4 collective-permute-start.12
  266.0 2.1 collective-permute-start.13
  268.1 1.3 collective-permute-start.14
  276.2 1.3 scatter_fusion.3
  278.2 270.6 %all-reduce.4.cloned.1.call-done = (f32[2,384,128]{2,1,0:T(8,128)}, f32[2,128,128]{2,1,0:T(8,128)}, f32[2,256,128]{2,1,0:T(8,128)}, f32[2,128,128]{2,1,0:T(8,128)}) async-done(((f32[2,384,128]{2,1,0:T(8,128)}, f32[2,128,128]{2,1,0:T(8,128)}, f32[2,256,128]{2,1,0:T(8,128)}, f32[2,128,128]{2,1,0:T(8,128)}), (f32[2,384,128]{2,1,0:T(8,128)}, f32[2,128,128]{2,1,0:T(8,128)}, f32[2,256,128]{2,1,0:T(8,128)}, ...) | async-done | bytes 917520 | tf_op jit(solution)/shard_map/psum | solution.py:138
  548.7 1.8 broadcast_multiply_fusion
  (319 shorter events, 55.0 us)
Async XLA Ops:
  7.2 29.5 %copy-start = (bf16[256,128]{1,0:T(8,128)(2,1)S(1)}, bf16[256,128]{1,0:T(8,128)(2,1)}, u32[]{:S(2)}) copy-start(bf16[256,128]{1,0:T(8,128)(2,1)} %param.19) | copy-start | bytes 196612
  7.2 541.6 %all-reduce.4.cloned.1.call-start = ((), (), s32[]{:S(2)}) async-start(), calls=%async_computation | async-start | bytes 1835008 | tf_op jit(solution)/shard_map/psum | solution.py:138
  11.1 30.0 %collective-permute-start.3 = (bf16[32,128]{1,0:T(8,128)(2,1)S(1)}, bf16[32,128]{1,0:T(8,128)(2,1)S(1)}, u32[]{:S(2)}, u32[]{:S(2)}) collective-permute-start(bf16[32,128]{1,0:T(8,128)(2,1)S(1)} %get-tuple-element.94), channel_id=1, source_target_pairs={{1,0},{2,1},{3,2},{4,3},{5,4},{6,5},{7,6},{9,8},{10,9},{11,10},{12... | collective-permute-start | bytes 24584 | tf_op jit(solution)/shard_map/ppermute | solution.py:20
  12.4 28.6 %collective-permute-start.1 = (bf16[32,128]{1,0:T(8,128)(2,1)S(1)}, bf16[32,128]{1,0:T(8,128)(2,1)S(1)}, u32[]{:S(2)}, u32[]{:S(2)}) collective-permute-start(bf16[32,128]{1,0:T(8,128)(2,1)S(1)} %get-tuple-element.95), channel_id=1, source_target_pairs={{0,504},{8,0},{16,8},{24,16},{32,24},{40,32},{48,40},{56,48},{64,5... | collective-permute-start | bytes 24584 | tf_op jit(solution)/shard_map/ppermute | solution.py:14
  21.2 19.8 %collective-permute-start = (bf16[32,128]{1,0:T(8,128)(2,1)S(1)}, bf16[32,128]{1,0:T(8,128)(2,1)S(1)}, u32[]{:S(2)}, u32[]{:S(2)}) collective-permute-start(bf16[32,128]{1,0:T(8,128)(2,1)S(1)} %get-tuple-element.96), channel_id=1, source_target_pairs={{0,8},{8,16},{16,24},{24,32},{32,40},{40,48},{48,56},{56,64},{64,7... | collective-permute-start | bytes 24584 | tf_op jit(solution)/shard_map/ppermute | solution.py:14
  23.1 17.9 %collective-permute-start.2 = (bf16[32,128]{1,0:T(8,128)(2,1)S(1)}, bf16[32,128]{1,0:T(8,128)(2,1)S(1)}, u32[]{:S(2)}, u32[]{:S(2)}) collective-permute-start(bf16[32,128]{1,0:T(8,128)(2,1)S(1)} %get-tuple-element.97), channel_id=1, source_target_pairs={{0,1},{1,2},{2,3},{3,4},{4,5},{5,6},{6,7},{8,9},{9,10},{10,11},{11... | collective-permute-start | bytes 24584 | tf_op jit(solution)/shard_map/ppermute | solution.py:20
  32.9 13.5 %copy-start.49 = (f32[128]{0:T(128)}, f32[128]{0:T(128)S(1)}, u32[]{:S(2)}) copy-start(f32[128]{0:T(128)S(1)} %get-tuple-element.112) | copy-start | bytes 1540
  32.9 47.4 %copy-start.51 = (f32[128]{0:T(128)}, f32[128]{0:T(128)S(1)}, u32[]{:S(2)}) copy-start(f32[128]{0:T(128)S(1)} %get-tuple-element.111) | copy-start | bytes 1540
  35.4 18.5 %copy-start.47 = (f32[128]{0:T(128)}, f32[128]{0:T(128)S(1)}, u32[]{:S(2)}) copy-start(f32[128]{0:T(128)S(1)} %get-tuple-element.108) | copy-start | bytes 1540
  55.2 19.2 %collective-permute-start.7 = (bf16[32,128]{0,1:T(8,128)(2,1)S(1)}, bf16[32,128]{0,1:T(8,128)(2,1)S(1)}, u32[]{:S(2)}, u32[]{:S(2)}) collective-permute-start(bf16[32,128]{0,1:T(8,128)(2,1)S(1)} %get-tuple-element.90), channel_id=1, source_target_pairs={{1,0},{2,1},{3,2},{4,3},{5,4},{6,5},{7,6},{9,8},{10,9},{11,10},{12... | collective-permute-start | bytes 24584 | tf_op jit(solution)/shard_map/ppermute | solution.py:20
  56.5 17.9 %collective-permute-start.5 = (bf16[32,128]{0,1:T(8,128)(2,1)S(1)}, bf16[32,128]{0,1:T(8,128)(2,1)S(1)}, u32[]{:S(2)}, u32[]{:S(2)}) collective-permute-start(bf16[32,128]{0,1:T(8,128)(2,1)S(1)} %get-tuple-element.91), channel_id=1, source_target_pairs={{0,504},{8,0},{16,8},{24,16},{32,24},{40,32},{48,40},{56,48},{64,5... | collective-permute-start | bytes 24584 | tf_op jit(solution)/shard_map/ppermute | solution.py:14
  64.4 10.0 %collective-permute-start.4 = (bf16[32,128]{0,1:T(8,128)(2,1)S(1)}, bf16[32,128]{0,1:T(8,128)(2,1)S(1)}, u32[]{:S(2)}, u32[]{:S(2)}) collective-permute-start(bf16[32,128]{0,1:T(8,128)(2,1)S(1)} %get-tuple-element.92), channel_id=1, source_target_pairs={{0,8},{8,16},{16,24},{24,32},{32,40},{40,48},{48,56},{56,64},{64,7... | collective-permute-start | bytes 24584 | tf_op jit(solution)/shard_map/ppermute | solution.py:14
  66.4 8.1 %collective-permute-start.6 = (bf16[32,128]{0,1:T(8,128)(2,1)S(1)}, bf16[32,128]{0,1:T(8,128)(2,1)S(1)}, u32[]{:S(2)}, u32[]{:S(2)}) collective-permute-start(bf16[32,128]{0,1:T(8,128)(2,1)S(1)} %get-tuple-element.93), channel_id=1, source_target_pairs={{0,1},{1,2},{2,3},{3,4},{4,5},{5,6},{6,7},{8,9},{9,10},{10,11},{11... | collective-permute-start | bytes 24584 | tf_op jit(solution)/shard_map/ppermute | solution.py:20
  81.1 6.9 %copy-start.64 = (bf16[2,128,128]{2,1,0:T(8,128)(2,1)S(1)}, bf16[2,128,128]{2,1,0:T(8,128)(2,1)}, u32[]{:S(2)}) copy-start(bf16[2,128,128]{2,1,0:T(8,128)(2,1)} %param.32) | copy-start | bytes 196612
  81.3 7.0 %copy-start.53 = (f32[128]{0:T(128)S(1)}, f32[128]{0:T(128)}, u32[]{:S(2)}) copy-start(f32[128]{0:T(128)} %get-tuple-element.107) | copy-start | bytes 1540
  107.1 21.7 %copy-start.21 = (bf16[256,128]{0,1:T(8,128)(2,1)S(1)}, bf16[256,128]{0,1:T(8,128)(2,1)}, u32[]{:S(2)}) copy-start(bf16[256,128]{0,1:T(8,128)(2,1)} %copy-done.20) | copy-start | bytes 196612
  107.1 21.7 %copy-start.26 = (bf16[256,128]{1,0:T(8,128)(2,1)S(1)}, bf16[256,128]{1,0:T(8,128)(2,1)}, u32[]{:S(2)}) copy-start(bf16[256,128]{1,0:T(8,128)(2,1)} %copy-done.25) | copy-start | bytes 196612
  113.3 19.9 %copy-start.54 = (s32[128]{0:T(128)S(1)}, s32[128]{0:T(128)}, u32[]{:S(2)}) copy-start(s32[128]{0:T(128)} %fusion.111) | copy-start | bytes 1540
  113.4 16.3 %collective-permute-start.8 = (f32[32,128]{0,1:T(8,128)}, f32[32,128]{0,1:T(8,128)S(1)}, u32[]{:S(2)}, u32[]{:S(2)}) collective-permute-start(f32[32,128]{0,1:T(8,128)} %get-tuple-element.86), channel_id=1, source_target_pairs={{0,8},{8,16},{16,24},{24,32},{32,40},{40,48},{48,56},{56,64},{64,7... | collective-permute-start | bytes 49160 | tf_op jit(solution)/shard_map/ppermute | solution.py:14
  115.3 14.5 %collective-permute-start.9 = (f32[32,128]{0,1:T(8,128)}, f32[32,128]{0,1:T(8,128)S(1)}, u32[]{:S(2)}, u32[]{:S(2)}) collective-permute-start(f32[32,128]{0,1:T(8,128)} %get-tuple-element.87), channel_id=1, source_target_pairs={{0,504},{8,0},{16,8},{24,16},{32,24},{40,32},{48,40},{56,48},{64,5... | collective-permute-start | bytes 49160 | tf_op jit(solution)/shard_map/ppermute | solution.py:14
  123.2 6.7 %collective-permute-start.10 = (f32[32,128]{0,1:T(8,128)}, f32[32,128]{0,1:T(8,128)S(1)}, u32[]{:S(2)}, u32[]{:S(2)}) collective-permute-start(f32[32,128]{0,1:T(8,128)} %get-tuple-element.88), channel_id=1, source_target_pairs={{0,1},{1,2},{2,3},{3,4},{4,5},{5,6},{6,7},{8,9},{9,10},{10,11},{11... | collective-permute-start | bytes 49160 | tf_op jit(solution)/shard_map/ppermute | solution.py:20
  127.4 5.6 %collective-permute-start.11 = (f32[32,128]{0,1:T(8,128)}, f32[32,128]{0,1:T(8,128)S(1)}, u32[]{:S(2)}, u32[]{:S(2)}) collective-permute-start(f32[32,128]{0,1:T(8,128)} %get-tuple-element.89), channel_id=1, source_target_pairs={{1,0},{2,1},{3,2},{4,3},{5,4},{6,5},{7,6},{9,8},{10,9},{11,10},{12... | collective-permute-start | bytes 49160 | tf_op jit(solution)/shard_map/ppermute | solution.py:20
  257.3 13.5 %copy-start.36 = (bf16[1,128,128]{2,1,0:T(8,128)(2,1)S(1)}, bf16[1,128,128]{2,1,0:T(8,128)(2,1)}, u32[]{:S(2)}) copy-start(bf16[1,128,128]{2,1,0:T(8,128)(2,1)} %fusion.11) | copy-start | bytes 98308
  257.3 13.5 %copy-start.38 = (bf16[1,128,128]{2,1,0:T(8,128)(2,1)S(1)}, bf16[1,128,128]{2,1,0:T(8,128)(2,1)}, u32[]{:S(2)}) copy-start(bf16[1,128,128]{2,1,0:T(8,128)(2,1)} %fusion.10) | copy-start | bytes 98308
  257.3 14.1 %copy-start.23 = (bf16[1,256,128]{2,1,0:T(8,128)(2,1)S(1)}, bf16[1,256,128]{2,1,0:T(8,128)(2,1)}, u32[]{:S(2)}) copy-start(bf16[1,256,128]{2,1,0:T(8,128)(2,1)} %fusion.7) | copy-start | bytes 196612
  257.3 14.1 %copy-start.24 = (bf16[1,256,128]{2,1,0:T(8,128)(2,1)S(1)}, bf16[1,256,128]{2,1,0:T(8,128)(2,1)}, u32[]{:S(2)}) copy-start(bf16[1,256,128]{2,1,0:T(8,128)(2,1)} %fusion.6) | copy-start | bytes 196612
  257.3 14.8 %copy-start.37 = (bf16[1,128,128]{2,1,0:T(8,128)(2,1)S(1)}, bf16[1,128,128]{2,1,0:T(8,128)(2,1)}, u32[]{:S(2)}) copy-start(bf16[1,128,128]{2,1,0:T(8,128)(2,1)} %fusion.9) | copy-start | bytes 98308
  263.5 9.3 %copy-start.17 = (bf16[1,384,128]{2,1,0:T(8,128)(2,1)S(1)}, bf16[1,384,128]{2,1,0:T(8,128)(2,1)}, u32[]{:S(2)}) copy-start(bf16[1,384,128]{2,1,0:T(8,128)(2,1)} %fusion.3) | copy-start | bytes 294916
  263.6 12.1 %collective-permute-start.12 = (f32[32,128]{0,1:T(8,128)S(1)}, f32[32,128]{0,1:T(8,128)S(1)}, u32[]{:S(2)}, u32[]{:S(2)}) collective-permute-start(f32[32,128]{0,1:T(8,128)S(1)} %get-tuple-element.82), channel_id=1, source_target_pairs={{0,8},{8,16},{16,24},{24,32},{32,40},{40,48},{48,56},{56,64},{64,7... | collective-permute-start | bytes 49160 | tf_op jit(solution)/shard_map/ppermute | solution.py:14
  266.0 9.7 %collective-permute-start.13 = (f32[32,128]{0,1:T(8,128)S(1)}, f32[32,128]{0,1:T(8,128)S(1)}, u32[]{:S(2)}, u32[]{:S(2)}) collective-permute-start(f32[32,128]{0,1:T(8,128)S(1)} %get-tuple-element.83), channel_id=1, source_target_pairs={{0,504},{8,0},{16,8},{24,16},{32,24},{40,32},{48,40},{56,48},{64,5... | collective-permute-start | bytes 49160 | tf_op jit(solution)/shard_map/ppermute | solution.py:14
  268.1 7.7 %collective-permute-start.14 = (f32[32,128]{0,1:T(8,128)S(1)}, f32[32,128]{0,1:T(8,128)S(1)}, u32[]{:S(2)}, u32[]{:S(2)}) collective-permute-start(f32[32,128]{0,1:T(8,128)S(1)} %get-tuple-element.84), channel_id=1, source_target_pairs={{0,1},{1,2},{2,3},{3,4},{4,5},{5,6},{6,7},{8,9},{9,10},{10,11},{11... | collective-permute-start | bytes 49160 | tf_op jit(solution)/shard_map/ppermute | solution.py:20
  269.4 6.7 %collective-permute-start.15 = (f32[32,128]{0,1:T(8,128)S(1)}, f32[32,128]{0,1:T(8,128)S(1)}, u32[]{:S(2)}, u32[]{:S(2)}) collective-permute-start(f32[32,128]{0,1:T(8,128)S(1)} %get-tuple-element.85), channel_id=1, source_target_pairs={{1,0},{2,1},{3,2},{4,3},{5,4},{6,5},{7,6},{9,8},{10,9},{11,10},{12... | collective-permute-start | bytes 49160 | tf_op jit(solution)/shard_map/ppermute | solution.py:20
  (61 other events, 143.5 us)
Sparse Core Ops, SparseCore 0:
  273.8 274.9 all-reduce.3
where the time goes:
time: 561 us; the launch traced here: 559 us
  waiting for transfers between devices  274 us (49%)
  blocking collectives  102 us (18%)
  other arithmetic  60 us (11%)
  starting transfers between devices  54.5 us (10%)
  local copies, waits for them, and re-layouts  39.7 us (7%)
  between operations  16.3 us (3%)
  matrix products  12.8 us (2%)
    psum x1, waiting for transfers between devices, per_device(): stacked_grads = lax.psum(stacked_grads, ('sector', 'span'))  271 us
    psum x1, blocking collectives, per_device(): stacked_grads = lax.psum(stacked_grads, ('sector', 'span'))  102 us
    ppermute x8, starting transfers between devices, passed_along(): lax.ppermute(array, axis, [(i, (i + by) % peers) for i in range(peers)])  34.8 us
    ppermute x8, starting transfers between devices, shifted(): lax.ppermute(value, axis, [(source, source + steps) for source in range(l...  19.6 us
    scatter-add x2, other arithmetic, tile_step(): jax.ops.segment_sum(live_mask[:, None] * new_edge_f, receiver_ids, num_se...  12.5 us
    scatter-add x2, other arithmetic, tile_step(): jnp.take(extended, sender_ids, axis=0)  12.4 us
    scatter-add x2, other arithmetic, tile_step(): jnp.take(own_half, receiver_ids, axis=0)  12.3 us
  transfers between devices with their start and end apart: 17, of which 3 were waited for; matrix products, arithmetic and copies ran while one was open for 4% of the time, Pallas kernels for 0%

commit v1 on v0

v1 whole, which is shorter than its diff:
```python
import jax
import jax.numpy as jnp
from jax import lax
from jax.experimental import pallas as pl
from jax.experimental.pallas import tpu as pltpu
from jax.sharding import PartitionSpec as P

F32, BF16 = jnp.float32, jnp.bfloat16
MESH = pl.DeviceIdType.MESH
STEPS = 2
EPS = 1e-05
Y, ZH, C, X, ZL = 8, 4, 2, 4, 2
NODES, SLOTS, D, HALO = 256, 1024, 128, 32
CHUNK = 256
AT_EF, AT_ES, AT_NF, AT_NS, AT_SMALL, ROWS = 0, 384, 512, 768, 896, 1024


def dot(a, b):
    return jnp.dot(a, b, preferred_element_type=F32)


def dot_first(a, b):
    return lax.dot_general(a, b, (((0,), (0,)), ((), ())), preferred_element_type=F32)


def dot_last(a, b):
    return lax.dot_general(a, b, (((1,), (1,)), ((), ())), preferred_element_type=F32)


def ones_where(mask):
    return jnp.where(mask, 1.0, 0.0).astype(BF16)


def activate(lin):
    sig = 0.5 * jnp.tanh(0.5 * lin) + 0.5
    act = lin * sig
    return act, sig + act * (1.0 - sig)


def normalized(proj):
    mean = jnp.mean(proj, axis=-1, keepdims=True)
    centred = proj - mean
    var = jnp.mean(centred * centred, axis=-1, keepdims=True)
    inv = lax.rsqrt(var + EPS)
    return centred * inv, inv


def normalized_back(dout, xhat, inv, gain):
    prod = dout * xhat
    dx = dout * gain
    mean = jnp.mean(dx, axis=-1, keepdims=True)
    along = jnp.mean(prod * gain, axis=-1, keepdims=True)
    return inv * (dx - mean - xhat * along), jnp.sum(prod, axis=0, keepdims=True)


def kernel(
    nodes, edges, snd, rcv, halo, counts, cot, ef, eb, es, eg, nf, nb, ns, ng,
    node_grad, edge_grad, o_ef, o_eb, o_es, o_eg, o_nf, o_nb, o_ns, o_ng,
    own_pick, rest, spread, hal_pad, h1, part, act_e, slope_e, xhat_e, inv_e, act_n, slope_n, xhat_n, inv_n,
    node_in, edge_new, de, dlin, dproj, dh,
    halo_out, halo_in, grads, got1, got2, mid, total,
    halo_ssem, halo_rsem, red_ssem, red_rsem,
):
    sector, span = lax.axis_index("sector"), lax.axis_index("span")
    n_sector, n_span = Y * ZH * C, X * ZL
    y, zh, c = sector // (ZH * C), lax.rem(sector // C, ZH), lax.rem(sector, C)
    x, zl = span // ZL, lax.rem(span, ZL)
    g1, g2 = ZH * X * C, Y * ZL
    me1, me2 = (zh * X + x) * C + c, y * ZL + zl
    unit = ROWS // g1

    def peer1(j):
        return ((y * ZH + j // (X * C)) * C + lax.rem(j, C), lax.rem(j // C, X) * ZL + zl)

    def peer2(j):
        return ((j // ZL * ZH + zh) * C + c, x * ZL + lax.rem(j, ZL))

    around = (
        (lax.rem(sector + n_sector - 1, n_sector), span),
        (lax.rem(sector + 1, n_sector), span),
        (sector, lax.rem(span + n_span - 1, n_span)),
        (sector, lax.rem(span + 1, n_span)),
    )

    barrier = pltpu.get_barrier_semaphore()
    for peer in around:
        pl.semaphore_signal(barrier, inc=1, device_id=peer, device_id_type=MESH)

    def greet1(k, _):
        pl.semaphore_signal(barrier, inc=1, device_id=peer1(lax.rem(me1 + k, g1)), device_id_type=MESH)
        return 0

    def greet2(k, _):
        pl.semaphore_signal(barrier, inc=1, device_id=peer2(lax.rem(me2 + k, g2)), device_id_type=MESH)
        return 0

    lax.fori_loop(1, g1, greet1, 0)
    lax.fori_loop(1, g2, greet2, 0)

    hal_pad[...] = jnp.zeros_like(hal_pad)
    hal_pad[0:4, 0:HALO] = halo[0].astype(F32)
    padded = hal_pad[...]
    lane = lax.broadcasted_iota(jnp.int32, (1, D), 1)
    flat = jnp.zeros((1, D), F32)
    for k in range(4):
        row = padded[k : k + 1, :] if k == 0 else pltpu.roll(padded, HALO * k, 1)[k : k + 1, :]
        flat = jnp.where((lane >= HALO * k) & (lane < HALO * (k + 1)), row, flat)
    lane_f = lax.broadcasted_iota(jnp.int32, (D, D), 1).astype(F32)
    down = jnp.broadcast_to(flat, (D, D)).T
    halo_pick = jnp.concatenate([ones_where(down == lane_f), ones_where(down == lane_f + D)], axis=1)
    halo_spread = ones_where(lax.broadcasted_iota(jnp.int32, (NODES, D), 0).astype(F32) == flat)

    row_id = lax.broadcasted_iota(jnp.int32, (4 * HALO, 1), 0)
    outside = ((row_id >= 2 * HALO) & (row_id < 3 * HALO) & (span == 0)) | (
        (row_id >= 3 * HALO) & (span == n_span - 1)
    )

    def exchange_start(t):
        for k in range(4):
            pltpu.make_async_remote_copy(
                src_ref=halo_out.at[t, pl.ds(k * HALO, HALO)],
                dst_ref=halo_in.at[t, pl.ds((k ^ 1) * HALO, HALO)],
                send_sem=halo_ssem.at[t],
                recv_sem=halo_rsem.at[t],
                device_id=around[k],
                device_id_type=MESH,
            ).start()

    def exchange_wait(t):
        pltpu.make_async_copy(halo_in.at[t], halo_in.at[t], halo_rsem.at[t]).wait()

    halo_out[0] = dot(halo_pick, nodes[...]).astype(BF16)
    pl.semaphore_wait(barrier, 4 + g1 - 1 + g2 - 1)
    exchange_start(0)

    used = counts[0]
    slot = lax.broadcasted_iota(jnp.int32, (SLOTS // D, D), 0) * D + lax.broadcasted_iota(
        jnp.int32, (SLOTS // D, D), 1
    )
    snd_f = jnp.where(slot < used, snd[...], -1).astype(F32)
    rcv_f = jnp.where(slot < used, rcv[...], -1).astype(F32)
    down_f = lax.broadcasted_iota(jnp.int32, (NODES + 4 * HALO, D), 0).astype(F32)
    for r in range(SLOTS // D):
        at = pl.ds(r * D, D)
        s_row, r_row = snd_f[r : r + 1, :], rcv_f[r : r + 1, :]
        spread[0:384, at] = ones_where(down_f == s_row)
        spread[384:640, at] = ones_where(down_f[0:256] == r_row)
        s_col = jnp.broadcast_to(s_row, (D, D)).T
        r_col = jnp.broadcast_to(r_row, (D, D)).T
        own_pick[at, 0:128] = ones_where(s_col == lane_f)
        own_pick[at, 128:256] = ones_where(s_col == lane_f + 128.0)
        own_pick[at, 256:384] = ones_where(r_col == lane_f)
        own_pick[at, 384:512] = ones_where(r_col == lane_f + 128.0)
        rest[at, 0:128] = ones_where(s_col == lane_f + 256.0)
    rest[:, 128:256] = edges[...]

    def forward(t):
        h = nodes[...] if t == 0 else h1[...]
        own_table = jnp.concatenate(
            [dot(h, ef[t, 0:128, :]).astype(BF16), dot(h, ef[t, 128:256, :]).astype(BF16)], axis=0
        )
        bias, gain = eb[t : t + 1, :], eg[t : t + 1, :]
        for i in range(SLOTS // CHUNK):
            at = pl.ds(i * CHUNK, CHUNK)
            part[at, :] = dot(own_pick[at, :], own_table) + bias
        exchange_wait(t)
        halo_in[t] = jnp.where(outside, 0.0, halo_in[t].astype(F32)).astype(BF16)
        rest_table = jnp.concatenate(
            [dot(halo_in[t], ef[t, 0:128, :]).astype(BF16), ef[t, 256:384, :]], axis=0
        )
        for i in range(SLOTS // CHUNK):
            at = pl.ds(i * CHUNK, CHUNK)
            lin = part[at, :] + dot(rest[at, :], rest_table)
            act, slope = activate(lin)
            act = act.astype(BF16)
            act_e[t, at, :] = act
            slope_e[t, at, :] = slope
            xhat, inv = normalized(dot(act, es[t]))
            xhat_e[t, at, :] = xhat
            inv_e[t, at, :] = inv
            new = (rest[at, 128:256].astype(F32) + xhat * gain).astype(BF16)
            edge_new[at, :] = new
        summed = dot(spread[384:640, :], edge_new[...]).astype(BF16)
        if t + 1 < STEPS:
            rest[:, 128:256] = edge_new[...]
        node_in[t, :, 0:128] = h
        node_in[t, :, 128:256] = summed
        act, slope = activate(dot(node_in[t], nf[t]) + nb[t : t + 1, :])
        act = act.astype(BF16)
        act_n[t] = act
        slope_n[t] = slope
        xhat, inv = normalized(dot(act, ns[t]))
        xhat_n[t] = xhat
        inv_n[t] = inv
        if t + 1 < STEPS:
            new_h = (h.astype(F32) + xhat * ng[t : t + 1, :]).astype(BF16)
            h1[...] = new_h
            halo_out[t + 1] = dot(halo_pick, new_h).astype(BF16)
            exchange_start(t + 1)

    def reduce_start(t):
        def send(k, _):
            j = lax.rem(me1 + k, g1)
            pltpu.make_async_remote_copy(
                src_ref=grads.at[t, pl.ds(pl.multiple_of(j * unit, unit), unit)],
                dst_ref=got1.at[t, k],
                send_sem=red_ssem.at[t, 0],
                recv_sem=red_rsem.at[t, 0],
                device_id=peer1(j),
                device_id_type=MESH,
            ).start()
            return 0

        lax.fori_loop(1, g1, send, 0)

    def reduce_middle(t):
        others = got1.at[t, pl.ds(1, g1 - 1)]
        pltpu.make_async_copy(others, others, red_rsem.at[t, 0]).wait()
        acc = grads[t, pl.ds(pl.multiple_of(me1 * unit, unit), unit), :].astype(F32)
        for k in range(1, g1):
            acc = acc + got1[t, k].astype(F32)
        acc = acc.astype(BF16)
        mid[t] = acc
        got2[t, me2] = acc

        def send(k, _):
            j = lax.rem(me2 + k, g2)
            pltpu.make_async_remote_copy(
                src_ref=mid.at[t],
                dst_ref=got2.at[t, me2],
                send_sem=red_ssem.at[t, 1],
                recv_sem=red_rsem.at[t, 1],
                device_id=peer2(j),
                device_id_type=MESH,
            ).start()
            return 0

        lax.fori_loop(1, g2, send, 0)

    def reduce_last(t):
        others = got2.at[t, pl.ds(1, g2 - 1)]
        pltpu.make_async_copy(others, others, red_rsem.at[t, 1]).wait()
        acc = got2[t, 0].astype(F32)
        for k in range(1, g2):
            acc = acc + got2[t, k].astype(F32)
        scale = jnp.float32(NODES * n_sector * n_span) ** (-0.5)
        mine = pl.ds(pl.multiple_of(me1 * unit, unit), unit)
        total[t, mine, :] = (acc * scale).astype(BF16)

        def send(k, _):
            j = lax.rem(me1 + k, g1)
            pltpu.make_async_remote_copy(
                src_ref=total.at[t, mine],
                dst_ref=total.at[t, mine],
                send_sem=red_ssem.at[t, 2],
                recv_sem=red_rsem.at[t, 2],
                device_id=peer1(j),
                device_id_type=MESH,
            ).start()
            return 0

        lax.fori_loop(1, g1, send, 0)

    def reduce_finish(t):
        others = total.at[t, pl.ds(unit, ROWS - unit)]
        pltpu.make_async_copy(others, others, red_rsem.at[t, 2]).wait()
        for ref, start, count in ((o_ef, AT_EF, 384), (o_es, AT_ES, 128), (o_nf, AT_NF, 256), (o_ns, AT_NS, 128)):
            ref[t] = total[t, start : start + count, :].astype(F32)
        small = total[t, AT_SMALL : AT_SMALL + 16, :].astype(F32)
        o_eb[t : t + 1, :] = small[0:1, :]
        o_eg[t : t + 1, :] = small[1:2, :]
        o_nb[t : t + 1, :] = small[2:3, :]
        o_ng[t : t + 1, :] = small[3:4, :]

    def reduce_sent(t):
        for phase, ref, count in ((0, got1, g1), (1, got2, g2), (2, got1, g1)):
            sent = ref.at[t, pl.ds(1, count - 1)]
            pltpu.make_async_copy(sent, sent, red_ssem.at[t, phase]).wait()

    def backward(t):
        last = t + 1 == STEPS
        h = nodes[...] if t == 0 else h1[...]
        dy = cot[...].astype(F32) if last else dh[...]
        dproj_n, dgain_n = normalized_back(dy, xhat_n[t], inv_n[t], ng[t : t + 1, :])
        dproj_n = dproj_n.astype(BF16)
        dlin_n = dot_last(dproj_n, ns[t]) * slope_n[t]
        dbias_n = jnp.sum(dlin_n, axis=0, keepdims=True)
        dlin_n = dlin_n.astype(BF16)
        dsummed = dot_last(dlin_n, nf[t, 128:256, :]).astype(BF16)
        dgain_e = jnp.zeros((1, D), F32)
        gain = eg[t : t + 1, :]
        for i in range(SLOTS // CHUNK):
            at = pl.ds(i * CHUNK, CHUNK)
            dnew = dot(own_pick[at, 256:512], dsummed)
            if not last:
                dnew = dnew + de[at, :]
            dp, dg = normalized_back(dnew, xhat_e[t, at, :], inv_e[t, at, :], gain)
            dgain_e = dgain_e + dg
            dp = dp.astype(BF16)
            dproj[at, :] = dp
            dl = (dot_last(dp, es[t]) * slope_e[t, at, :]).astype(BF16)
            dlin[at, :] = dl
            dold = dnew + dot_last(dl, ef[t, 256:384, :])
            if last:
                de[at, :] = dold
            else:
                edge_grad[at, :] = dold.astype(BF16)
        sums = dot(spread[...], dlin[...])
        sums_b = sums.astype(BF16)
        dbias_e = jnp.sum(sums[384:640], axis=0, keepdims=True)
        dhalo = dot_last(sums_b[256:384], ef[t, 0:128, :])
        halo_out[STEPS + t] = jnp.where(outside, 0.0, dhalo).astype(BF16)
        exchange_start(STEPS + t)
        grads[t, AT_EF : AT_EF + 128, :] = (
            dot_first(h, sums_b[0:256]) + dot_first(halo_in[t], sums_b[256:384])
        ).astype(BF16)
        grads[t, AT_EF + 128 : AT_EF + 256, :] = dot_first(h, sums_b[384:640]).astype(BF16)
        old = edges[...] if t == 0 else rest[:, 128:256]
        grads[t, AT_EF + 256 : AT_EF + 384, :] = dot_first(old, dlin[...]).astype(BF16)
        grads[t, AT_ES : AT_ES + 128, :] = dot_first(act_e[t], dproj[...]).astype(BF16)
        grads[t, AT_NF : AT_NF + 256, :] = dot_first(node_in[t], dlin_n).astype(BF16)
        grads[t, AT_NS : AT_NS + 128, :] = dot_first(act_n[t], dproj_n).astype(BF16)
        grads[t, AT_SMALL : AT_SMALL + 128, :] = jnp.concatenate(
            [dbias_e, dgain_e, dbias_n, dgain_n, jnp.zeros((124, D), F32)], axis=0
        ).astype(BF16)
        reduce_start(t)
        own = (
            dy
            + dot_last(dlin_n, nf[t, 0:128, :])
            + dot_last(sums_b[0:256], ef[t, 0:128, :])
            + dot_last(sums_b[384:640], ef[t, 128:256, :])
        )
        exchange_wait(STEPS + t)
        own = (own + dot(halo_spread, halo_in[STEPS + t])).astype(BF16)
        if t == 0:
            node_grad[...] = own
        else:
            dh[...] = own.astype(F32)

    forward(0)
    forward(1)
    backward(1)
    reduce_middle(1)
    backward(0)
    reduce_last(1)
    reduce_middle(0)
    reduce_finish(1)
    reduce_last(0)
    reduce_finish(0)
    for t in range(STEPS):
        reduce_sent(t)
    for t in range(2 * STEPS):
        pltpu.make_async_copy(halo_out.at[t], halo_out.at[t], halo_ssem.at[t]).wait()


def per_device(
    node_latents, edge_latents, senders, receivers, halo_rows, counts, cotangent,
    edge_first, edge_bias, edge_second, edge_gain, node_first, node_bias, node_second, node_gain,
):
    g1, g2 = ZH * X * C, Y * ZL
    unit = ROWS // g1
    vmem, smem = pl.BlockSpec(memory_space=pltpu.VMEM), pl.BlockSpec(memory_space=pltpu.SMEM)
    weights = (edge_first, edge_bias, edge_second, edge_gain, node_first, node_bias, node_second, node_gain)
    return pl.pallas_call(
        kernel,
        out_shape=(
            jax.ShapeDtypeStruct((NODES, D), BF16),
            jax.ShapeDtypeStruct((SLOTS, D), BF16),
            *(jax.ShapeDtypeStruct(w.shape, F32) for w in weights),
        ),
        in_specs=[vmem] * 5 + [smem] + [vmem] * 9,
        out_specs=[vmem] * 10,
        scratch_shapes=[
            pltpu.VMEM((SLOTS, 512), BF16),
            pltpu.VMEM((SLOTS, 256), BF16),
            pltpu.VMEM((640, SLOTS), BF16),
            pltpu.VMEM((8, D), F32),
            pltpu.VMEM((NODES, D), BF16),
            pltpu.VMEM((SLOTS, D), F32),
            pltpu.VMEM((STEPS, SLOTS, D), BF16),
            pltpu.VMEM((STEPS, SLOTS, D), F32),
            pltpu.VMEM((STEPS, SLOTS, D), F32),
            pltpu.VMEM((STEPS, SLOTS, 1), F32),
            pltpu.VMEM((STEPS, NODES, D), BF16),
            pltpu.VMEM((STEPS, NODES, D), F32),
            pltpu.VMEM((STEPS, NODES, D), F32),
            pltpu.VMEM((STEPS, NODES, 1), F32),
            pltpu.VMEM((STEPS, NODES, 256), BF16),
            pltpu.VMEM((SLOTS, D), BF16),
            pltpu.VMEM((SLOTS, D), F32),
            pltpu.VMEM((SLOTS, D), BF16),
            pltpu.VMEM((SLOTS, D), BF16),
            pltpu.VMEM((NODES, D), F32),
            pltpu.VMEM((2 * STEPS, 4 * HALO, D), BF16),
            pltpu.VMEM((2 * STEPS, 4 * HALO, D), BF16),
            pltpu.VMEM((STEPS, ROWS, D), BF16),
            pltpu.VMEM((STEPS, g1, unit, D), BF16),
            pltpu.VMEM((STEPS, g2, unit, D), BF16),
            pltpu.VMEM((STEPS, unit, D), BF16),
            pltpu.VMEM((STEPS, ROWS, D), BF16),
            pltpu.SemaphoreType.DMA((2 * STEPS,)),
            pltpu.SemaphoreType.DMA((2 * STEPS,)),
            pltpu.SemaphoreType.DMA((STEPS, 3)),
            pltpu.SemaphoreType.DMA((STEPS, 3)),
        ],
        compiler_params=pltpu.CompilerParams(
            collective_id=0, has_side_effects=True, vmem_limit_bytes=40 * 1024 * 1024
        ),
    )(
        node_latents, edge_latents, senders.reshape(SLOTS // D, D), receivers.reshape(SLOTS // D, D),
        halo_rows, counts, cotangent, *weights,
    )


def solution(mesh):
    tile = P(("sector", "span"))
    rows = P(("sector", "span"), None)
    return jax.shard_map(
        per_device,
        mesh=mesh,
        in_specs=(rows, rows, tile, tile, P(("sector", "span"), None, None), tile, rows) + (P(),) * 8,
        out_specs=(rows, rows) + (P(),) * 8,
        check_vma=False,
    )
```

time: 561 us -> 86.9 us (0.15)
  waiting for transfers between devices: 274 us -> 0 us
  blocking collectives: 102 us -> 0 us
  Pallas kernels: 0 us -> 68.4 us
  other arithmetic: 60 us -> 0 us
  starting transfers between devices: 54.5 us -> 0 us
  local copies, waits for them, and re-layouts: 39.7 us -> 16.5 us
  between operations: 16.3 us -> 1.35 us
  matrix products: 12.8 us -> 0 us
    psum x1 -> x0, waiting for transfers between devices: 271 us -> none  [per_device(): stacked_grads = lax.psum(stacked_grads, ('sector', 'span'))]
    psum x1 -> x0, blocking collectives: 102 us -> none  [per_device(): stacked_grads = lax.psum(stacked_grads, ('sector', 'span'))]
    pallas_call x0 -> x1, Pallas kernels: none -> 68.4 us  [per_device(): pl.pallas_call(kernel, out_shape=(jax.ShapeDtypeStruct((NODES, D), BF16),...]
    ppermute x16 -> x0, starting transfers between devices: 54.4 us -> none  [the longest x8 34.8 us: passed_along(): lax.ppermute(array, axis, [(i, (i + by) % peers) for i in range(peers)])]
    scatter-add x8 -> x0, other arithmetic: 40.1 us -> none  [the longest x2 12.5 us: tile_step(): jax.ops.segment_sum(live_mask[:, None] * new_edge_f, receiver_ids, num_se...]
    gather x13 -> x0, local copies, waits for them, and re-layouts: 20.7 us -> none  [the longest x3 6.56 us: tile_step(): jnp.take(extended, sender_ids, axis=0)]
    dot_general x24 -> x0, matrix products: 12.8 us -> none  [the longest x12 7.43 us: network(): jnp.dot(activated, second.astype(jnp.bfloat16), preferred_element_type=jn...]
    unnamed x160 -> x38, local copies, waits for them, and re-layouts: 10.1 us -> 16.5 us
  transfers between devices with their start and end apart: 17 -> 0, of which waited for: 3 -> 0; matrix products, arithmetic and copies ran while one was open for 4% -> 0% of each run, Pallas kernels for 0% -> 0%
where the time goes in v1:
time: 86.9 us; the launch traced here: 86.3 us
  Pallas kernels  68.4 us (79%)
  local copies, waits for them, and re-layouts  16.5 us (19%)
  between operations  1.35 us (2%)
    pallas_call x1, Pallas kernels, per_device(): pl.pallas_call(kernel, out_shape=(jax.ShapeDtypeStruct((NODES, D), BF16),...  68.4 us
    unnamed x38, local copies, waits for them, and re-layouts  16.5 us

profile of v1, /device:TPU:1, one launch (start us, length us, event | category | flops | bytes accessed | tf_op | source)
XLA Modules:
  0.0 86.3 jit_solution(9516375829455710023)
XLA Ops:
  0.6 0.0 copy-start.7
  1.3 0.0 copy-start.10
  1.3 0.0 copy-done.7
  1.3 0.7 copy-done.10
  2.0 0.0 copy-start
  2.0 0.9 %copy-done = bf16[1024,128]{1,0:T(8,128)(2,1)S(1)} copy-done((bf16[1024,128]{1,0:T(8,128)(2,1)S(1)}, bf16[1024,128]{1,0:T(8,128)(2,1)}, u32[]{:S(2)}) %copy-start) | copy-done | bytes 262168
  2.9 0.0 copy-start.1
  3.0 0.9 %copy-done.1 = bf16[2,384,128]{2,1,0:T(8,128)(2,1)S(1)} copy-done((bf16[2,384,128]{2,1,0:T(8,128)(2,1)S(1)}, bf16[2,384,128]{2,1,0:T(8,128)(2,1)}, u32[]{:S(2)}) %copy-start.1) | copy-done | bytes 196632
  3.9 0.0 copy-start.2
  3.9 0.9 %copy-done.2 = bf16[2,256,128]{2,1,0:T(8,128)(2,1)S(1)} copy-done((bf16[2,256,128]{2,1,0:T(8,128)(2,1)S(1)}, bf16[2,256,128]{2,1,0:T(8,128)(2,1)}, u32[]{:S(2)}) %copy-start.2) | copy-done | bytes 131096
  4.8 0.0 copy-start.3
  4.8 0.8 copy-done.3
  5.6 0.0 copy-start.4
  5.6 0.8 copy-done.4
  6.5 0.8 copy-done.5
  7.3 0.8 copy-done.6
  8.1 0.7 copy-done.8
  8.8 0.7 copy-done.9
  9.5 0.7 copy-done.11
  10.2 0.7 copy-done.12
  10.9 0.7 copy-done.13
  11.5 68.4 %shard_map.222 = (bf16[256,128]{1,0:T(8,128)(2,1)S(1)}, bf16[1024,128]{1,0:T(8,128)(2,1)S(1)}, f32[2,384,128]{2,1,0:T(8,128)S(1)}, f32[2,128]{1,0:T(2,128)S(1)},...) custom-call(bf16[256,128]{1,0:T(8,128)(2,1)S(1)} %copy-done.3, ...), custom_call_target="tpu_custom_call" | custom-call | tf_op jit(solution)/shard_map/pallas_call | solution.py:364
  80.0 0.6 copy.36
  80.6 0.7 copy.37
  81.3 0.7 copy.38
  82.1 0.6 copy.39
  82.6 0.7 copy.40
  83.3 0.6 copy.41
  83.8 0.7 copy.42
  84.5 0.6 copy.43
  85.1 0.7 copy.44
  85.8 0.6 copy.45
  (7 shorter events, 0.0 us)
Async XLA Ops:
  0.6 0.7 copy-start.7
  1.3 0.7 copy-start.10
  2.0 0.9 %copy-start = (bf16[1024,128]{1,0:T(8,128)(2,1)S(1)}, bf16[1024,128]{1,0:T(8,128)(2,1)}, u32[]{:S(2)}) copy-start(bf16[1024,128]{1,0:T(8,128)(2,1)} %edges.1) | copy-start | bytes 786436
  2.9 0.9 %copy-start.1 = (bf16[2,384,128]{2,1,0:T(8,128)(2,1)S(1)}, bf16[2,384,128]{2,1,0:T(8,128)(2,1)}, u32[]{:S(2)}) copy-start(bf16[2,384,128]{2,1,0:T(8,128)(2,1)} %ef.1) | copy-start | bytes 589828
  3.9 0.9 %copy-start.2 = (bf16[2,256,128]{2,1,0:T(8,128)(2,1)S(1)}, bf16[2,256,128]{2,1,0:T(8,128)(2,1)}, u32[]{:S(2)}) copy-start(bf16[2,256,128]{2,1,0:T(8,128)(2,1)} %nf.1) | copy-start | bytes 393220
  4.8 0.8 copy-start.3
  5.6 0.8 copy-start.4
  6.5 0.8 copy-start.5
  7.3 0.8 copy-start.6
  8.1 0.7 copy-start.8
  8.8 0.7 copy-start.9
  9.5 0.7 copy-start.11
  10.2 0.7 copy-start.12
  10.9 0.7 copy-start.13

commit v2 on v1

--- a/solution.py
+++ b/solution.py
@@ -9,7 +9,7 @@
 MESH = pl.DeviceIdType.MESH
 STEPS = 2
 EPS = 1e-05
-Y, ZH, C, X, ZL = 8, 4, 2, 4, 2
+YH, YL, ZH, C, X, ZL = 4, 2, 4, 2, 4, 2
 NODES, SLOTS, D, HALO = 256, 1024, 128, 32
 CHUNK = 256
 AT_EF, AT_ES, AT_NF, AT_NS, AT_SMALL, ROWS = 0, 384, 512, 768, 896, 1024
@@ -54,26 +54,32 @@
 
 
 def kernel(
-    nodes, edges, snd, rcv, halo, counts, cot, ef, eb, es, eg, nf, nb, ns, ng,
-    node_grad, edge_grad, o_ef, o_eb, o_es, o_eg, o_nf, o_nb, o_ns, o_ng,
+    *refs,
+):
+    sources, counts, outs, here, refs = refs[:5] + refs[6:15], refs[5], refs[15:18], refs[18:32], refs[32:]
+    nodes, edges, snd, rcv, halo, cot, ef, eb, es, eg, nf, nb, ns, ng = here
+    node_grad, edge_grad, total = outs
+    (
     own_pick, rest, spread, hal_pad, h1, part, act_e, slope_e, xhat_e, inv_e, act_n, slope_n, xhat_n, inv_n,
     node_in, edge_new, de, dlin, dproj, dh,
-    halo_out, halo_in, grads, got1, got2, mid, total,
-    halo_ssem, halo_rsem, red_ssem, red_rsem,
-):
+    halo_out, halo_in, grads, got1, got2, mid,
+    in_sem, halo_ssem, halo_rsem, red_ssem, red_rsem,
+    ) = refs
     sector, span = lax.axis_index("sector"), lax.axis_index("span")
-    n_sector, n_span = Y * ZH * C, X * ZL
-    y, zh, c = sector // (ZH * C), lax.rem(sector // C, ZH), lax.rem(sector, C)
+    n_sector, n_span = YH * YL * ZH * C, X * ZL
+    yh, yl = sector // (YL * ZH * C), lax.rem(sector // (ZH * C), YL)
+    zh, c = lax.rem(sector // C, ZH), lax.rem(sector, C)
     x, zl = span // ZL, lax.rem(span, ZL)
-    g1, g2 = ZH * X * C, Y * ZL
-    me1, me2 = (zh * X + x) * C + c, y * ZL + zl
+    g1, g2 = YL * ZL * X * C, YH * ZH
+    me1, me2 = ((yl * ZL + zl) * X + x) * C + c, yh * ZH + zh
     unit = ROWS // g1
 
     def peer1(j):
-        return ((y * ZH + j // (X * C)) * C + lax.rem(j, C), lax.rem(j // C, X) * ZL + zl)
+        py, pz = j // (ZL * X * C), lax.rem(j // (X * C), ZL)
+        return (((yh * YL + py) * ZH + zh) * C + lax.rem(j, C), lax.rem(j // C, X) * ZL + pz)
 
     def peer2(j):
-        return ((j // ZL * ZH + zh) * C + c, x * ZL + lax.rem(j, ZL))
+        return (((j // ZH * YL + yl) * ZH + lax.rem(j, ZH)) * C + c, span)
 
     around = (
         (lax.rem(sector + n_sector - 1, n_sector), span),
@@ -96,6 +102,14 @@
 
     lax.fori_loop(1, g1, greet1, 0)
     lax.fori_loop(1, g2, greet2, 0)
+
+    loads = [pltpu.make_async_copy(a, b, in_sem.at[i]) for i, (a, b) in enumerate(zip(sources, here))]
+    first = (4, 0, 2, 3, 1)
+    rest_loads = [i for i in range(14) if i not in first]
+    for i in (*first, *rest_loads):
+        loads[i].start()
+    loads[4].wait()
+    loads[0].wait()
 
     hal_pad[...] = jnp.zeros_like(hal_pad)
     hal_pad[0:4, 0:HALO] = halo[0].astype(F32)
@@ -133,6 +147,8 @@
     pl.semaphore_wait(barrier, 4 + g1 - 1 + g2 - 1)
     exchange_start(0)
 
+    for i in first[2:]:
+        loads[i].wait()
     used = counts[0]
     slot = lax.broadcasted_iota(jnp.int32, (SLOTS // D, D), 0) * D + lax.broadcasted_iota(
         jnp.int32, (SLOTS // D, D), 1
@@ -153,6 +169,8 @@
         own_pick[at, 384:512] = ones_where(r_col == lane_f + 128.0)
         rest[at, 0:128] = ones_where(s_col == lane_f + 256.0)
     rest[:, 128:256] = edges[...]
+    for i in rest_loads:
+        loads[i].wait()
 
     def forward(t):
         h = nodes[...] if t == 0 else h1[...]
@@ -264,13 +282,6 @@
     def reduce_finish(t):
         others = total.at[t, pl.ds(unit, ROWS - unit)]
         pltpu.make_async_copy(others, others, red_rsem.at[t, 2]).wait()
-        for ref, start, count in ((o_ef, AT_EF, 384), (o_es, AT_ES, 128), (o_nf, AT_NF, 256), (o_ns, AT_NS, 128)):
-            ref[t] = total[t, start : start + count, :].astype(F32)
-        small = total[t, AT_SMALL : AT_SMALL + 16, :].astype(F32)
-        o_eb[t : t + 1, :] = small[0:1, :]
-        o_eg[t : t + 1, :] = small[1:2, :]
-        o_nb[t : t + 1, :] = small[2:3, :]
-        o_ng[t : t + 1, :] = small[3:4, :]
 
     def reduce_sent(t):
         for phase, ref, count in ((0, got1, g1), (1, got2, g2), (2, got1, g1)):
@@ -308,9 +319,14 @@
         sums = dot(spread[...], dlin[...])
         sums_b = sums.astype(BF16)
         dbias_e = jnp.sum(sums[384:640], axis=0, keepdims=True)
-        dhalo = dot_last(sums_b[256:384], ef[t, 0:128, :])
-        halo_out[STEPS + t] = jnp.where(outside, 0.0, dhalo).astype(BF16)
-        exchange_start(STEPS + t)
+
+        def send_back():
+            dhalo = dot_last(sums_b[256:384], ef[t, 0:128, :])
+            halo_out[STEPS + t] = jnp.where(outside, 0.0, dhalo).astype(BF16)
+            exchange_start(STEPS + t)
+
+        if last:
+            send_back()
         grads[t, AT_EF : AT_EF + 128, :] = (
             dot_first(h, sums_b[0:256]) + dot_first(halo_in[t], sums_b[256:384])
         ).astype(BF16)
@@ -323,29 +339,33 @@
         grads[t, AT_SMALL : AT_SMALL + 128, :] = jnp.concatenate(
             [dbias_e, dgain_e, dbias_n, dgain_n, jnp.zeros((124, D), F32)], axis=0
         ).astype(BF16)
-        reduce_start(t)
+        if not last:
+            reduce_start(t)
+            send_back()
         own = (
             dy
             + dot_last(dlin_n, nf[t, 0:128, :])
             + dot_last(sums_b[0:256], ef[t, 0:128, :])
             + dot_last(sums_b[384:640], ef[t, 128:256, :])
         )
+        if not last:
+            reduce_middle(1)
         exchange_wait(STEPS + t)
         own = (own + dot(halo_spread, halo_in[STEPS + t])).astype(BF16)
-        if t == 0:
+        if last:
+            reduce_start(t)
+            dh[...] = own.astype(F32)
+        else:
             node_grad[...] = own
-        else:
-            dh[...] = own.astype(F32)
 
     forward(0)
     forward(1)
     backward(1)
-    reduce_middle(1)
     backward(0)
+    reduce_middle(0)
     reduce_last(1)
-    reduce_middle(0)
+    reduce_last(0)
     reduce_finish(1)
-    reduce_last(0)
     reduce_finish(0)
     for t in range(STEPS):
         reduce_sent(t)
@@ -353,24 +373,51 @@
         pltpu.make_async_copy(halo_out.at[t], halo_out.at[t], halo_ssem.at[t]).wait()
 
 
+def finish(node_grad, edge_grad, total, *refs):
+    outs, wide, small, sem = refs[:10], refs[10], refs[11], refs[12]
+    copies = [pltpu.make_async_copy(edge_grad, outs[1], sem.at[0]), pltpu.make_async_copy(node_grad, outs[0], sem.at[1])]
+    for copy in copies:
+        copy.start()
+    big = ((2, AT_EF, 384), (4, AT_ES, 128), (6, AT_NF, 256), (8, AT_NS, 128))
+    for out, start, count in big:
+        wide[:, start : start + count, :] = total[:, start : start + count, :].astype(F32)
+        copy = pltpu.make_async_copy(wide.at[:, pl.ds(start, count), :], outs[out], sem.at[out])
+        copy.start()
+        copies.append(copy)
+    for k, out in enumerate((3, 5, 7, 9)):
+        for t in range(STEPS):
+            small[k, t : t + 1, :] = total[t, AT_SMALL : AT_SMALL + 16, :].astype(F32)[k : k + 1, :]
+        copy = pltpu.make_async_copy(small.at[k], outs[out], sem.at[out])
+        copy.start()
+        copies.append(copy)
+    for copy in copies:
+        copy.wait()
+
+
 def per_device(
     node_latents, edge_latents, senders, receivers, halo_rows, counts, cotangent,
     edge_first, edge_bias, edge_second, edge_gain, node_first, node_bias, node_second, node_gain,
 ):
-    g1, g2 = ZH * X * C, Y * ZL
+    g1, g2 = YL * ZL * X * C, YH * ZH
     unit = ROWS // g1
-    vmem, smem = pl.BlockSpec(memory_space=pltpu.VMEM), pl.BlockSpec(memory_space=pltpu.SMEM)
+    vmem, anywhere = pl.BlockSpec(memory_space=pltpu.VMEM), pl.BlockSpec(memory_space=pl.ANY)
+    smem, hbm = pl.BlockSpec(memory_space=pltpu.SMEM), pl.BlockSpec(memory_space=pltpu.HBM)
     weights = (edge_first, edge_bias, edge_second, edge_gain, node_first, node_bias, node_second, node_gain)
-    return pl.pallas_call(
+    args = (
+        node_latents, edge_latents, senders.reshape(SLOTS // D, D), receivers.reshape(SLOTS // D, D),
+        halo_rows, counts, cotangent, *weights,
+    )
+    parts = pl.pallas_call(
         kernel,
         out_shape=(
             jax.ShapeDtypeStruct((NODES, D), BF16),
             jax.ShapeDtypeStruct((SLOTS, D), BF16),
-            *(jax.ShapeDtypeStruct(w.shape, F32) for w in weights),
+            jax.ShapeDtypeStruct((STEPS, ROWS, D), BF16),
         ),
-        in_specs=[vmem] * 5 + [smem] + [vmem] * 9,
-        out_specs=[vmem] * 10,
+        in_specs=[smem if i == 5 else hbm for i in range(15)],
+        out_specs=[vmem] * 3,
         scratch_shapes=[
+            *(pltpu.VMEM(a.shape, a.dtype) for i, a in enumerate(args) if i != 5),
             pltpu.VMEM((SLOTS, 512), BF16),
             pltpu.VMEM((SLOTS, 256), BF16),
             pltpu.VMEM((640, SLOTS), BF16),
@@ -397,7 +444,7 @@
             pltpu.VMEM((STEPS, g1, unit, D), BF16),
             pltpu.VMEM((STEPS, g2, unit, D), BF16),
             pltpu.VMEM((STEPS, unit, D), BF16),
-            pltpu.VMEM((STEPS, ROWS, D), BF16),
+            pltpu.SemaphoreType.DMA((14,)),
             pltpu.SemaphoreType.DMA((2 * STEPS,)),
             pltpu.SemaphoreType.DMA((2 * STEPS,)),
             pltpu.SemaphoreType.DMA((STEPS, 3)),
@@ -406,10 +453,25 @@
         compiler_params=pltpu.CompilerParams(
             collective_id=0, has_side_effects=True, vmem_limit_bytes=40 * 1024 * 1024
         ),
-    )(
-        node_latents, edge_latents, senders.reshape(SLOTS // D, D), receivers.reshape(SLOTS // D, D),
-        halo_rows, counts, cotangent, *weights,
-    )
+        name="steps",
+    )(*(a if i == 5 else pltpu.with_memory_space_constraint(a, pltpu.HBM) for i, a in enumerate(args)))
+    return pl.pallas_call(
+        finish,
+        out_shape=(
+            jax.ShapeDtypeStruct((NODES, D), BF16),
+            jax.ShapeDtypeStruct((SLOTS, D), BF16),
+            *(jax.ShapeDtypeStruct(w.shape, F32) for w in weights),
+        ),
+        in_specs=[vmem] * 3,
+        out_specs=[anywhere] * 10,
+        scratch_shapes=[
+            pltpu.VMEM((STEPS, ROWS, D), F32),
+            pltpu.VMEM((4, STEPS, D), F32),
+            pltpu.SemaphoreType.DMA((10,)),
+        ],
+        compiler_params=pltpu.CompilerParams(vmem_limit_bytes=40 * 1024 * 1024),
+        name="finish",
+    )(*parts)
 
 
 def solution(mesh):

time: 86.9 us -> 60.6 us (0.70)
  local copies, waits for them, and re-layouts: 16.5 us -> 0 us
  Pallas kernels: 68.4 us -> 59.2 us
    unnamed x38 -> x0, local copies, waits for them, and re-layouts: 16.5 us -> none
    pallas_call x1, Pallas kernels: 68.4 us -> 58.1 us  [per_device(): pl.pallas_call(kernel, out_shape=(jax.ShapeDtypeStruct((NODES, D), BF16),...]
    pallas_call x0 -> x1, Pallas kernels: none -> 1.12 us  [per_device(): pl.pallas_call(finish, out_shape=(jax.ShapeDtypeStruct((NODES, D), BF16),...]
where the time goes in v2:
time: 60.6 us; the launch traced here: 60.5 us
  Pallas kernels  59.2 us (98%)
  between operations  1.3 us (2%)
    pallas_call x1, Pallas kernels, per_device(): pl.pallas_call(kernel, out_shape=(jax.ShapeDtypeStruct((NODES, D), BF16),...  58.1 us

profile of v2, /device:TPU:1, one launch (start us, length us, event | category | flops | bytes accessed | tf_op | source)
XLA Modules:
  0.0 60.5 jit_solution(15889378968763144919)
XLA Ops:
  1.3 58.1 %steps.1 = (bf16[256,128]{1,0:T(8,128)(2,1)S(1)}, bf16[1024,128]{1,0:T(8,128)(2,1)S(1)}, bf16[2,1024,128]{2,1,0:T(8,128)(2,1)S(1)}) custom-call(bf16[256,128]{1,0:T(8,128)(2,1)} %refs_0_.1, bf16[1024,128]{1,0:T(8,128)(2,1)} %refs_1_.1, s32[8,128]{1,0:T(8,128)} %bitcast.2, s32[8,128]{1,0:T(8,128)} %bitcast.3, s32[1,4,32]{2,1,0:T(4,128)} %refs_4_.1, ...), custom_call_target="tpu_custom_call" | custom-call | tf_op jit(solution)/shard_map/steps/pallas_call | solution.py:410
  59.4 1.1 %finish.1 = (bf16[256,128]{1,0:T(8,128)(2,1)}, bf16[1024,128]{1,0:T(8,128)(2,1)}, f32[2,384,128]{2,1,0:T(8,128)}, f32[2,128]{1,0:T(2,128)}, f32[2,128,128]{2,1,0...) custom-call(bf16[256,128]{1,0:T(8,128)(2,1)S(1)} %get-tuple-element., ...), custom_call_target="tpu_custom_call" | custom-call | tf_op jit(solution)/shard_map/finish/pallas_call | solution.py:458

commit v3 on v2

--- a/solution.py
+++ b/solution.py
@@ -12,7 +12,10 @@
 YH, YL, ZH, C, X, ZL = 4, 2, 4, 2, 4, 2
 NODES, SLOTS, D, HALO = 256, 1024, 128, 32
 CHUNK = 256
-AT_EF, AT_ES, AT_NF, AT_NS, AT_SMALL, ROWS = 0, 384, 512, 768, 896, 1024
+STEP1, NODE0, EDGE0 = 0, 1, 2
+ROWS = (1024, 512, 512)
+BASE = (0, 1024, 1536)
+SMALL = (896, 384)
 
 
 def dot(a, b):
@@ -62,8 +65,8 @@
     (
     own_pick, rest, spread, hal_pad, h1, part, act_e, slope_e, xhat_e, inv_e, act_n, slope_n, xhat_n, inv_n,
     node_in, edge_new, de, dlin, dproj, dh,
-    halo_out, halo_in, grads, got1, got2, mid,
-    in_sem, halo_ssem, halo_rsem, red_ssem, red_rsem,
+    halo_out, halo_in, grads, mid, got1_a, got1_b, got1_c, got2_a, got2_b, got2_c,
+    in_sem, halo_ssem, halo_rsem, red_ssem, red_rsem, ready,
     ) = refs
     sector, span = lax.axis_index("sector"), lax.axis_index("span")
     n_sector, n_span = YH * YL * ZH * C, X * ZL
@@ -72,7 +75,8 @@
     x, zl = span // ZL, lax.rem(span, ZL)
     g1, g2 = YL * ZL * X * C, YH * ZH
     me1, me2 = ((yl * ZL + zl) * X + x) * C + c, yh * ZH + zh
-    unit = ROWS // g1
+    units = tuple(n // g1 for n in ROWS)
+    got1, got2 = (got1_a, got1_b, got1_c), (got2_a, got2_b, got2_c)
 
     def peer1(j):
         py, pz = j // (ZL * X * C), lax.rem(j // (X * C), ZL)
@@ -96,12 +100,10 @@
         pl.semaphore_signal(barrier, inc=1, device_id=peer1(lax.rem(me1 + k, g1)), device_id_type=MESH)
         return 0
 
-    def greet2(k, _):
-        pl.semaphore_signal(barrier, inc=1, device_id=peer2(lax.rem(me2 + k, g2)), device_id_type=MESH)
-        return 0
-
     lax.fori_loop(1, g1, greet1, 0)
-    lax.fori_loop(1, g2, greet2, 0)
+    lines = [peer2(lax.rem(yh + k, YH) * ZH + zh) for k in range(1, YH)]
+    for peer in lines + [peer2(yh * ZH + lax.rem(zh + k, ZH)) for k in range(1, ZH)]:
+        pl.semaphore_signal(barrier, inc=1, device_id=peer, device_id_type=MESH)
 
     loads = [pltpu.make_async_copy(a, b, in_sem.at[i]) for i, (a, b) in enumerate(zip(sources, here))]
     first = (4, 0, 2, 3, 1)
@@ -144,8 +146,10 @@
         pltpu.make_async_copy(halo_in.at[t], halo_in.at[t], halo_rsem.at[t]).wait()
 
     halo_out[0] = dot(halo_pick, nodes[...]).astype(BF16)
-    pl.semaphore_wait(barrier, 4 + g1 - 1 + g2 - 1)
+    pl.semaphore_wait(barrier, 4 + g1 - 1 + YH - 1 + ZH - 1)
     exchange_start(0)
+    for peer in lines:
+        pl.semaphore_signal(ready, inc=1, device_id=peer, device_id_type=MESH)
 
     for i in first[2:]:
         loads[i].wait()
@@ -216,14 +220,77 @@
             halo_out[t + 1] = dot(halo_pick, new_h).astype(BF16)
             exchange_start(t + 1)
 
-    def reduce_start(t):
+    def reduce_start(i, held=None, only=None):
+        unit = units[i]
+
+        def copy(j):
+            pltpu.make_async_remote_copy(
+                src_ref=grads.at[pl.ds(pl.multiple_of(BASE[i] + j * unit, unit), unit)],
+                dst_ref=got1[i].at[me1],
+                send_sem=red_ssem.at[i, 0],
+                recv_sem=red_rsem.at[i, 0],
+                device_id=peer1(j),
+                device_id_type=MESH,
+            ).start()
+
+        def send(k, _):
+            j = lax.rem(me1 + k, g1)
+            if held is None:
+                copy(j)
+            else:
+                pl.when(j != held)(lambda: copy(j))
+            return 0
+
+        if only is None:
+            lax.fori_loop(1, g1, send, 0)
+        else:
+            pl.when(me1 != only)(lambda: copy(only))
+
+    def reduce_middle(i):
+        unit = units[i]
+        others = got1[i].at[pl.ds(1, g1 - 1)]
+        pltpu.make_async_copy(others, others, red_rsem.at[i, 0]).wait()
+        got1[i][me1] = grads[pl.ds(pl.multiple_of(BASE[i] + me1 * unit, unit), unit), :]
+        acc = got1[i][0].astype(F32)
+        for k in range(1, g1):
+            acc = acc + got1[i][k].astype(F32)
+        acc = acc.astype(BF16)
+        block = pl.ds(BASE[i] // g1, unit)
+        mid[block, :] = acc
+        got2[i][me2] = acc
+
+        def send(k, _):
+            j = lax.rem(me2 + k, g2)
+            pltpu.make_async_remote_copy(
+                src_ref=mid.at[block],
+                dst_ref=got2[i].at[me2],
+                send_sem=red_ssem.at[i, 1],
+                recv_sem=red_rsem.at[i, 1],
+                device_id=peer2(j),
+                device_id_type=MESH,
+            ).start()
+            return 0
+
+        lax.fori_loop(1, g2, send, 0)
+
+    def reduce_last(i):
+        unit = units[i]
+        others = got2[i].at[pl.ds(1, g2 - 1)]
+        pltpu.make_async_copy(others, others, red_rsem.at[i, 1]).wait()
+        acc = got2[i][0].astype(F32)
+        for k in range(1, g2):
+            acc = acc + got2[i][k].astype(F32)
+        scale = jnp.float32(NODES * n_sector * n_span) ** (-0.5)
+        mine = pl.ds(pl.multiple_of(BASE[i] + me1 * unit, unit), unit)
+        total[mine, :] = (acc * scale).astype(BF16)
+
         def send(k, _):
             j = lax.rem(me1 + k, g1)
             pltpu.make_async_remote_copy(
-                src_ref=grads.at[t, pl.ds(pl.multiple_of(j * unit, unit), unit)],
-                dst_ref=got1.at[t, k],
-                send_sem=red_ssem.at[t, 0],
-                recv_sem=red_rsem.at[t, 0],
+                src_ref=total.at[mine],
+                dst_ref=total.at[mine],
+                send_sem=red_ssem.at[i, 2],
+                recv_sem=red_rsem.at[i, 2],
                 device_id=peer1(j),
                 device_id_type=MESH,
             ).start()
@@ -231,62 +298,14 @@
 
         lax.fori_loop(1, g1, send, 0)
 
-    def reduce_middle(t):
-        others = got1.at[t, pl.ds(1, g1 - 1)]
-        pltpu.make_async_copy(others, others, red_rsem.at[t, 0]).wait()
-        acc = grads[t, pl.ds(pl.multiple_of(me1 * unit, unit), unit), :].astype(F32)
-        for k in range(1, g1):
-            acc = acc + got1[t, k].astype(F32)
-        acc = acc.astype(BF16)
-        mid[t] = acc
-        got2[t, me2] = acc
-
-        def send(k, _):
-            j = lax.rem(me2 + k, g2)
-            pltpu.make_async_remote_copy(
-                src_ref=mid.at[t],
-                dst_ref=got2.at[t, me2],
-                send_sem=red_ssem.at[t, 1],
-                recv_sem=red_rsem.at[t, 1],
-                device_id=peer2(j),
-                device_id_type=MESH,
-            ).start()
-            return 0
-
-        lax.fori_loop(1, g2, send, 0)
-
-    def reduce_last(t):
-        others = got2.at[t, pl.ds(1, g2 - 1)]
-        pltpu.make_async_copy(others, others, red_rsem.at[t, 1]).wait()
-        acc = got2[t, 0].astype(F32)
-        for k in range(1, g2):
-            acc = acc + got2[t, k].astype(F32)
-        scale = jnp.float32(NODES * n_sector * n_span) ** (-0.5)
-        mine = pl.ds(pl.multiple_of(me1 * unit, unit), unit)
-        total[t, mine, :] = (acc * scale).astype(BF16)
-
-        def send(k, _):
-            j = lax.rem(me1 + k, g1)
-            pltpu.make_async_remote_copy(
-                src_ref=total.at[t, mine],
-                dst_ref=total.at[t, mine],
-                send_sem=red_ssem.at[t, 2],
-                recv_sem=red_rsem.at[t, 2],
-                device_id=peer1(j),
-                device_id_type=MESH,
-            ).start()
-            return 0
-
-        lax.fori_loop(1, g1, send, 0)
-
-    def reduce_finish(t):
-        others = total.at[t, pl.ds(unit, ROWS - unit)]
-        pltpu.make_async_copy(others, others, red_rsem.at[t, 2]).wait()
-
-    def reduce_sent(t):
-        for phase, ref, count in ((0, got1, g1), (1, got2, g2), (2, got1, g1)):
-            sent = ref.at[t, pl.ds(1, count - 1)]
-            pltpu.make_async_copy(sent, sent, red_ssem.at[t, phase]).wait()
+    def reduce_finish(i):
+        others = total.at[pl.ds(BASE[i], ROWS[i] - units[i])]
+        pltpu.make_async_copy(others, others, red_rsem.at[i, 2]).wait()
+
+    def reduce_sent(i):
+        for phase, ref, count in ((0, got1[i], g1), (1, got2[i], g2), (2, got1[i], g1)):
+            sent = ref.at[pl.ds(1, count - 1)]
+            pltpu.make_async_copy(sent, sent, red_ssem.at[i, phase]).wait()
 
     def backward(t):
         last = t + 1 == STEPS
@@ -298,6 +317,20 @@
         dbias_n = jnp.sum(dlin_n, axis=0, keepdims=True)
         dlin_n = dlin_n.astype(BF16)
         dsummed = dot_last(dlin_n, nf[t, 128:256, :]).astype(BF16)
+        node_at = BASE[STEP1] + 512 if last else BASE[NODE0]
+        small_at = BASE[STEP1] + SMALL[STEP1] if last else BASE[NODE0] + SMALL[NODE0]
+        held = SMALL[NODE0] // units[NODE0]
+
+        def node_grads():
+            grads[node_at : node_at + 256, :] = dot_first(node_in[t], dlin_n).astype(BF16)
+            grads[node_at + 256 : node_at + 384, :] = dot_first(act_n[t], dproj_n).astype(BF16)
+
+        small_rows = 128 if last else units[NODE0]
+        if not last:
+            node_grads()
+            if small_rows < 128:
+                grads[small_at + small_rows : small_at + 128, :] = jnp.zeros((128 - small_rows, D), BF16)
+            reduce_start(NODE0, held=held)
         dgain_e = jnp.zeros((1, D), F32)
         gain = eg[t : t + 1, :]
         for i in range(SLOTS // CHUNK):
@@ -325,22 +358,25 @@
             halo_out[STEPS + t] = jnp.where(outside, 0.0, dhalo).astype(BF16)
             exchange_start(STEPS + t)
 
+        edge_at = BASE[STEP1] if last else BASE[EDGE0]
         if last:
             send_back()
-        grads[t, AT_EF : AT_EF + 128, :] = (
+        grads[edge_at : edge_at + 128, :] = (
             dot_first(h, sums_b[0:256]) + dot_first(halo_in[t], sums_b[256:384])
         ).astype(BF16)
-        grads[t, AT_EF + 128 : AT_EF + 256, :] = dot_first(h, sums_b[384:640]).astype(BF16)
+        grads[edge_at + 128 : edge_at + 256, :] = dot_first(h, sums_b[384:640]).astype(BF16)
         old = edges[...] if t == 0 else rest[:, 128:256]
-        grads[t, AT_EF + 256 : AT_EF + 384, :] = dot_first(old, dlin[...]).astype(BF16)
-        grads[t, AT_ES : AT_ES + 128, :] = dot_first(act_e[t], dproj[...]).astype(BF16)
-        grads[t, AT_NF : AT_NF + 256, :] = dot_first(node_in[t], dlin_n).astype(BF16)
-        grads[t, AT_NS : AT_NS + 128, :] = dot_first(act_n[t], dproj_n).astype(BF16)
-        grads[t, AT_SMALL : AT_SMALL + 128, :] = jnp.concatenate(
-            [dbias_e, dgain_e, dbias_n, dgain_n, jnp.zeros((124, D), F32)], axis=0
+        grads[edge_at + 256 : edge_at + 384, :] = dot_first(old, dlin[...]).astype(BF16)
+        grads[edge_at + 384 : edge_at + 512, :] = dot_first(act_e[t], dproj[...]).astype(BF16)
+        grads[small_at : small_at + small_rows, :] = jnp.concatenate(
+            [dbias_e, dgain_e, dbias_n, dgain_n, jnp.zeros((small_rows - 4, D), F32)], axis=0
         ).astype(BF16)
-        if not last:
-            reduce_start(t)
+        if last:
+            node_grads()
+            reduce_start(STEP1)
+        else:
+            reduce_start(EDGE0)
+            reduce_start(NODE0, only=held)
             send_back()
         own = (
             dy
@@ -349,11 +385,12 @@
             + dot_last(sums_b[384:640], ef[t, 128:256, :])
         )
         if not last:
-            reduce_middle(1)
+            pl.semaphore_wait(ready, YH - 1)
+            reduce_middle(STEP1)
+            reduce_middle(NODE0)
         exchange_wait(STEPS + t)
         own = (own + dot(halo_spread, halo_in[STEPS + t])).astype(BF16)
         if last:
-            reduce_start(t)
             dh[...] = own.astype(F32)
         else:
             node_grad[...] = own
@@ -362,13 +399,13 @@
     forward(1)
     backward(1)
     backward(0)
-    reduce_middle(0)
-    reduce_last(1)
-    reduce_last(0)
-    reduce_finish(1)
-    reduce_finish(0)
-    for t in range(STEPS):
-        reduce_sent(t)
+    reduce_middle(EDGE0)
+    for i in (STEP1, NODE0, EDGE0):
+        reduce_last(i)
+    for i in (STEP1, NODE0, EDGE0):
+        reduce_finish(i)
+    for i in (STEP1, NODE0, EDGE0):
+        reduce_sent(i)
     for t in range(2 * STEPS):
         pltpu.make_async_copy(halo_out.at[t], halo_out.at[t], halo_ssem.at[t]).wait()
 
@@ -378,15 +415,21 @@
     copies = [pltpu.make_async_copy(edge_grad, outs[1], sem.at[0]), pltpu.make_async_copy(node_grad, outs[0], sem.at[1])]
     for copy in copies:
         copy.start()
-    big = ((2, AT_EF, 384), (4, AT_ES, 128), (6, AT_NF, 256), (8, AT_NS, 128))
-    for out, start, count in big:
-        wide[:, start : start + count, :] = total[:, start : start + count, :].astype(F32)
-        copy = pltpu.make_async_copy(wide.at[:, pl.ds(start, count), :], outs[out], sem.at[out])
+    where = ((BASE[EDGE0], BASE[STEP1]), (BASE[NODE0], BASE[STEP1] + 512))
+    for out, part, first, count in ((2, 0, 0, 384), (4, 0, 384, 128), (6, 1, 0, 256), (8, 1, 256, 128)):
+        to = part * 512 + first
+        for t in range(STEPS):
+            start = where[part][t] + first
+            wide[t, to : to + count, :] = total[start : start + count, :].astype(F32)
+        copy = pltpu.make_async_copy(wide.at[:, pl.ds(to, count), :], outs[out], sem.at[out])
         copy.start()
         copies.append(copy)
+    smalls = (BASE[NODE0] + SMALL[NODE0], BASE[STEP1] + SMALL[STEP1])
+    for t in range(STEPS):
+        rows = total[smalls[t] : smalls[t] + 16, :].astype(F32)
+        for k in range(4):
+            small[k, t : t + 1, :] = rows[k : k + 1, :]
     for k, out in enumerate((3, 5, 7, 9)):
-        for t in range(STEPS):
-            small[k, t : t + 1, :] = total[t, AT_SMALL : AT_SMALL + 16, :].astype(F32)[k : k + 1, :]
         copy = pltpu.make_async_copy(small.at[k], outs[out], sem.at[out])
         copy.start()
         copies.append(copy)
@@ -399,7 +442,6 @@
     edge_first, edge_bias, edge_second, edge_gain, node_first, node_bias, node_second, node_gain,
 ):
     g1, g2 = YL * ZL * X * C, YH * ZH
-    unit = ROWS // g1
     vmem, anywhere = pl.BlockSpec(memory_space=pltpu.VMEM), pl.BlockSpec(memory_space=pl.ANY)
     smem, hbm = pl.BlockSpec(memory_space=pltpu.SMEM), pl.BlockSpec(memory_space=pltpu.HBM)
     weights = (edge_first, edge_bias, edge_second, edge_gain, node_first, node_bias, node_second, node_gain)
@@ -412,7 +454,7 @@
         out_shape=(
             jax.ShapeDtypeStruct((NODES, D), BF16),
             jax.ShapeDtypeStruct((SLOTS, D), BF16),
-            jax.ShapeDtypeStruct((STEPS, ROWS, D), BF16),
+            jax.ShapeDtypeStruct((sum(ROWS), D), BF16),
         ),
         in_specs=[smem if i == 5 else hbm for i in range(15)],
         out_specs=[vmem] * 3,
@@ -440,15 +482,16 @@
             pltpu.VMEM((NODES, D), F32),
             pltpu.VMEM((2 * STEPS, 4 * HALO, D), BF16),
             pltpu.VMEM((2 * STEPS, 4 * HALO, D), BF16),
-            pltpu.VMEM((STEPS, ROWS, D), BF16),
-            pltpu.VMEM((STEPS, g1, unit, D), BF16),
-            pltpu.VMEM((STEPS, g2, unit, D), BF16),
-            pltpu.VMEM((STEPS, unit, D), BF16),
+            pltpu.VMEM((sum(ROWS), D), BF16),
+            pltpu.VMEM((sum(ROWS) // g1, D), BF16),
+            *(pltpu.VMEM((g1, n // g1, D), BF16) for n in ROWS),
+            *(pltpu.VMEM((g2, n // g1, D), BF16) for n in ROWS),
             pltpu.SemaphoreType.DMA((14,)),
             pltpu.SemaphoreType.DMA((2 * STEPS,)),
             pltpu.SemaphoreType.DMA((2 * STEPS,)),
-            pltpu.SemaphoreType.DMA((STEPS, 3)),
-            pltpu.SemaphoreType.DMA((STEPS, 3)),
+            pltpu.SemaphoreType.DMA((3, 3)),
+            pltpu.SemaphoreType.DMA((3, 3)),
+            pltpu.SemaphoreType.REGULAR,
         ],
         compiler_params=pltpu.CompilerParams(
             collective_id=0, has_side_effects=True, vmem_limit_bytes=40 * 1024 * 1024
@@ -465,7 +508,7 @@
         in_specs=[vmem] * 3,
         out_specs=[anywhere] * 10,
         scratch_shapes=[
-            pltpu.VMEM((STEPS, ROWS, D), F32),
+            pltpu.VMEM((STEPS, 896, D), F32),
             pltpu.VMEM((4, STEPS, D), F32),
             pltpu.SemaphoreType.DMA((10,)),
         ],

time: 60.6 us -> 59.6 us (0.983)
  Pallas kernels: 59.2 us -> 58.1 us
    pallas_call x1, Pallas kernels: 58.1 us -> 57 us  [per_device(): pl.pallas_call(kernel, out_shape=(jax.ShapeDtypeStruct((NODES, D), BF16),...]
where the time goes in v3:
time: 59.6 us; the launch traced here: 59.4 us
  Pallas kernels  58.1 us (97%)
  between operations  1.3 us (2%)
    pallas_call x1, Pallas kernels, per_device(): pl.pallas_call(kernel, out_shape=(jax.ShapeDtypeStruct((NODES, D), BF16),...  57 us

profile of v3, /device:TPU:1, one launch (start us, length us, event | category | flops | bytes accessed | tf_op | source)
XLA Modules:
  0.0 59.4 jit_solution(2974764223388922312)
XLA Ops:
  1.3 57.0 %steps.1 = (bf16[256,128]{1,0:T(8,128)(2,1)S(1)}, bf16[1024,128]{1,0:T(8,128)(2,1)S(1)}, bf16[2048,128]{1,0:T(8,128)(2,1)S(1)}) custom-call(bf16[256,128]{1,0:T(8,128)(2,1)} %refs_0_.1, bf16[1024,128]{1,0:T(8,128)(2,1)} %refs_1_.1, s32[8,128]{1,0:T(8,128)} %bitcast.2, s32[8,128]{1,0:T(8,128)} %bitcast.3, s32[1,4,32]{2,1,0:T(4,128)} %refs_4_.1, ...), custom_call_target="tpu_custom_call" | custom-call | tf_op jit(solution)/shard_map/steps/pallas_call | solution.py:452
  58.3 1.1 %finish.1 = (bf16[256,128]{1,0:T(8,128)(2,1)}, bf16[1024,128]{1,0:T(8,128)(2,1)}, f32[2,384,128]{2,1,0:T(8,128)}, f32[2,128]{1,0:T(2,128)}, f32[2,128,128]{2,1,0...) custom-call(bf16[256,128]{1,0:T(8,128)(2,1)S(1)} %get-tuple-element., ...), custom_call_target="tpu_custom_call" | custom-call | tf_op jit(solution)/shard_map/finish/pallas_call | solution.py:501

commit v4 on v3

--- a/solution.py
+++ b/solution.py
@@ -1,3 +1,5 @@
+import functools
+
 import jax
 import jax.numpy as jnp
 from jax import lax
@@ -78,12 +80,23 @@
     units = tuple(n // g1 for n in ROWS)
     got1, got2 = (got1_a, got1_b, got1_c), (got2_a, got2_b, got2_c)
 
-    def peer1(j):
-        py, pz = j // (ZL * X * C), lax.rem(j // (X * C), ZL)
-        return (((yh * YL + py) * ZH + zh) * C + lax.rem(j, C), lax.rem(j // C, X) * ZL + pz)
-
-    def peer2(j):
-        return (((j // ZH * YL + yl) * ZH + lax.rem(j, ZH)) * C + c, span)
+    def turned(at, size):
+        return [at] + [lax.rem(at + k, size) for k in range(1, size)]
+
+    yls, zls, xs, cs = turned(yl, YL), turned(zl, ZL), turned(x, X), turned(c, C)
+    yhs, zhs = turned(yh, YH), turned(zh, ZH)
+    offsets1 = [(a, b, d, e) for a in range(YL) for b in range(ZL) for d in range(X) for e in range(C)][1:]
+    offsets1.sort(key=lambda o: -(o[0] + o[1] + min(o[2], X - o[2]) + 0.5 * o[3]))
+    peers1 = [
+        (
+            ((yls[a] * ZL + zls[b]) * X + xs[d]) * C + cs[e],
+            (((yh * YL + yls[a]) * ZH + zh) * C + cs[e], xs[d] * ZL + zls[b]),
+        )
+        for a, b, d, e in offsets1
+    ]
+    offsets2 = [(a, b) for a in range(YH) for b in range(ZH)][1:]
+    offsets2.sort(key=lambda o: -(min(o[0], YH - o[0]) + min(o[1], ZH - o[1])))
+    peers2 = [(((yhs[a] * YL + yl) * ZH + zhs[b]) * C + c, span) for a, b in offsets2]
 
     around = (
         (lax.rem(sector + n_sector - 1, n_sector), span),
@@ -96,13 +109,9 @@
     for peer in around:
         pl.semaphore_signal(barrier, inc=1, device_id=peer, device_id_type=MESH)
 
-    def greet1(k, _):
-        pl.semaphore_signal(barrier, inc=1, device_id=peer1(lax.rem(me1 + k, g1)), device_id_type=MESH)
-        return 0
-
-    lax.fori_loop(1, g1, greet1, 0)
-    lines = [peer2(lax.rem(yh + k, YH) * ZH + zh) for k in range(1, YH)]
-    for peer in lines + [peer2(yh * ZH + lax.rem(zh + k, ZH)) for k in range(1, ZH)]:
+    lines = [peer for peer, (a, b) in zip(peers2, offsets2) if b == 0]
+    greeted = [peer for _, peer in peers1] + [peer for peer, (a, b) in zip(peers2, offsets2) if a == 0 or b == 0]
+    for peer in greeted:
         pl.semaphore_signal(barrier, inc=1, device_id=peer, device_id_type=MESH)
 
     loads = [pltpu.make_async_copy(a, b, in_sem.at[i]) for i, (a, b) in enumerate(zip(sources, here))]
@@ -146,7 +155,7 @@
         pltpu.make_async_copy(halo_in.at[t], halo_in.at[t], halo_rsem.at[t]).wait()
 
     halo_out[0] = dot(halo_pick, nodes[...]).astype(BF16)
-    pl.semaphore_wait(barrier, 4 + g1 - 1 + YH - 1 + ZH - 1)
+    pl.semaphore_wait(barrier, 4 + len(greeted))
     exchange_start(0)
     for peer in lines:
         pl.semaphore_signal(ready, inc=1, device_id=peer, device_id_type=MESH)
@@ -223,28 +232,26 @@
     def reduce_start(i, held=None, only=None):
         unit = units[i]
 
-        def copy(j):
+        def copy(j, peer):
             pltpu.make_async_remote_copy(
                 src_ref=grads.at[pl.ds(pl.multiple_of(BASE[i] + j * unit, unit), unit)],
                 dst_ref=got1[i].at[me1],
                 send_sem=red_ssem.at[i, 0],
                 recv_sem=red_rsem.at[i, 0],
-                device_id=peer1(j),
+                device_id=peer,
                 device_id_type=MESH,
             ).start()
 
-        def send(k, _):
-            j = lax.rem(me1 + k, g1)
+        if only is not None:
+            at = only // (ZL * X * C), only // (X * C) % ZL, only // C % X, only % C
+            peer = (((yh * YL + at[0]) * ZH + zh) * C + at[3], at[2] * ZL + at[1])
+            pl.when(me1 != only)(lambda: copy(only, peer))
+            return
+        for j, peer in peers1:
             if held is None:
-                copy(j)
+                copy(j, peer)
             else:
-                pl.when(j != held)(lambda: copy(j))
-            return 0
-
-        if only is None:
-            lax.fori_loop(1, g1, send, 0)
-        else:
-            pl.when(me1 != only)(lambda: copy(only))
+                pl.when(j != held)(functools.partial(copy, j, peer))
 
     def reduce_middle(i):
         unit = units[i]
@@ -259,19 +266,15 @@
         mid[block, :] = acc
         got2[i][me2] = acc
 
-        def send(k, _):
-            j = lax.rem(me2 + k, g2)
+        for peer in peers2:
             pltpu.make_async_remote_copy(
                 src_ref=mid.at[block],
                 dst_ref=got2[i].at[me2],
                 send_sem=red_ssem.at[i, 1],
                 recv_sem=red_rsem.at[i, 1],
-                device_id=peer2(j),
+                device_id=peer,
                 device_id_type=MESH,
             ).start()
-            return 0
-
-        lax.fori_loop(1, g2, send, 0)
 
     def reduce_last(i):
         unit = units[i]
@@ -284,19 +287,15 @@
         mine = pl.ds(pl.multiple_of(BASE[i] + me1 * unit, unit), unit)
         total[mine, :] = (acc * scale).astype(BF16)
 
-        def send(k, _):
-            j = lax.rem(me1 + k, g1)
+        for _, peer in peers1:
             pltpu.make_async_remote_copy(
                 src_ref=total.at[mine],
                 dst_ref=total.at[mine],
                 send_sem=red_ssem.at[i, 2],
                 recv_sem=red_rsem.at[i, 2],
-                device_id=peer1(j),
+                device_id=peer,
                 device_id_type=MESH,
             ).start()
-            return 0
-
-        lax.fori_loop(1, g1, send, 0)
 
     def reduce_finish(i):
         others = total.at[pl.ds(BASE[i], ROWS[i] - units[i])]

time: 59.6 us -> 57.1 us (0.958)
  Pallas kernels: 58.1 us -> 55.7 us
    pallas_call x1, Pallas kernels: 57 us -> 54.5 us  [per_device(): pl.pallas_call(kernel, out_shape=(jax.ShapeDtypeStruct((NODES, D), BF16),...]
where the time goes in v4:
time: 57.1 us; the launch traced here: 57 us
  Pallas kernels  55.7 us (98%)
  between operations  1.3 us (2%)
    pallas_call x1, Pallas kernels, per_device(): pl.pallas_call(kernel, out_shape=(jax.ShapeDtypeStruct((NODES, D), BF16),...  54.5 us

profile of v4, /device:TPU:1, one launch (start us, length us, event | category | flops | bytes accessed | tf_op | source)
XLA Modules:
  0.0 57.0 jit_solution(2600004703774818974)
XLA Ops:
  1.3 54.5 %steps.1 = (bf16[256,128]{1,0:T(8,128)(2,1)S(1)}, bf16[1024,128]{1,0:T(8,128)(2,1)S(1)}, bf16[2048,128]{1,0:T(8,128)(2,1)S(1)}) custom-call(bf16[256,128]{1,0:T(8,128)(2,1)} %refs_0_.1, bf16[1024,128]{1,0:T(8,128)(2,1)} %refs_1_.1, s32[8,128]{1,0:T(8,128)} %bitcast.2, s32[8,128]{1,0:T(8,128)} %bitcast.3, s32[1,4,32]{2,1,0:T(4,128)} %refs_4_.1, ...), custom_call_target="tpu_custom_call" | custom-call | tf_op jit(solution)/shard_map/steps/pallas_call | solution.py:451
  55.9 1.1 %finish.1 = (bf16[256,128]{1,0:T(8,128)(2,1)}, bf16[1024,128]{1,0:T(8,128)(2,1)}, f32[2,384,128]{2,1,0:T(8,128)}, f32[2,128]{1,0:T(2,128)}, f32[2,128,128]{2,1,0...) custom-call(bf16[256,128]{1,0:T(8,128)(2,1)S(1)} %get-tuple-element., ...), custom_call_target="tpu_custom_call" | custom-call | tf_op jit(solution)/shard_map/finish/pallas_call | solution.py:500

commit v5 on v4

--- a/solution.py
+++ b/solution.py
@@ -13,7 +13,7 @@
 EPS = 1e-05
 YH, YL, ZH, C, X, ZL = 4, 2, 4, 2, 4, 2
 NODES, SLOTS, D, HALO = 256, 1024, 128, 32
-CHUNK = 256
+CHUNK = 512
 STEP1, NODE0, EDGE0 = 0, 1, 2
 ROWS = (1024, 512, 512)
 BASE = (0, 1024, 1536)
@@ -42,20 +42,20 @@
     return act, sig + act * (1.0 - sig)
 
 
+def centred(weight):
+    weight = weight.astype(F32)
+    return weight - jnp.mean(weight, axis=-1, keepdims=True)
+
+
 def normalized(proj):
-    mean = jnp.mean(proj, axis=-1, keepdims=True)
-    centred = proj - mean
-    var = jnp.mean(centred * centred, axis=-1, keepdims=True)
-    inv = lax.rsqrt(var + EPS)
-    return centred * inv, inv
+    inv = lax.rsqrt(jnp.mean(proj * proj, axis=-1, keepdims=True) + EPS)
+    return proj * inv, inv
 
 
 def normalized_back(dout, xhat, inv, gain):
     prod = dout * xhat
-    dx = dout * gain
-    mean = jnp.mean(dx, axis=-1, keepdims=True)
     along = jnp.mean(prod * gain, axis=-1, keepdims=True)
-    return inv * (dx - mean - xhat * along), jnp.sum(prod, axis=0, keepdims=True)
+    return inv * (dout * gain - xhat * along), jnp.sum(prod, axis=0, keepdims=True)
 
 
 def kernel(
@@ -67,7 +67,7 @@
     (
     own_pick, rest, spread, hal_pad, h1, part, act_e, slope_e, xhat_e, inv_e, act_n, slope_n, xhat_n, inv_n,
     node_in, edge_new, de, dlin, dproj, dh,
-    halo_out, halo_in, grads, mid, got1_a, got1_b, got1_c, got2_a, got2_b, got2_c,
+    es_c, ns_c, halo_out, halo_in, grads, mid, got1_a, got1_b, got1_c, got2_a, got2_b, got2_c,
     in_sem, halo_ssem, halo_rsem, red_ssem, red_rsem, ready,
     ) = refs
     sector, span = lax.axis_index("sector"), lax.axis_index("span")
@@ -185,6 +185,10 @@
     for i in rest_loads:
         loads[i].wait()
 
+    for t in range(STEPS):
+        es_c[t] = centred(es[t]).astype(BF16)
+        ns_c[t] = centred(ns[t]).astype(BF16)
+
     def forward(t):
         h = nodes[...] if t == 0 else h1[...]
         own_table = jnp.concatenate(
@@ -206,7 +210,7 @@
             act = act.astype(BF16)
             act_e[t, at, :] = act
             slope_e[t, at, :] = slope
-            xhat, inv = normalized(dot(act, es[t]))
+            xhat, inv = normalized(dot(act, es_c[t]))
             xhat_e[t, at, :] = xhat
             inv_e[t, at, :] = inv
             new = (rest[at, 128:256].astype(F32) + xhat * gain).astype(BF16)
@@ -220,7 +224,7 @@
         act = act.astype(BF16)
         act_n[t] = act
         slope_n[t] = slope
-        xhat, inv = normalized(dot(act, ns[t]))
+        xhat, inv = normalized(dot(act, ns_c[t]))
         xhat_n[t] = xhat
         inv_n[t] = inv
         if t + 1 < STEPS:
@@ -312,7 +316,7 @@
         dy = cot[...].astype(F32) if last else dh[...]
         dproj_n, dgain_n = normalized_back(dy, xhat_n[t], inv_n[t], ng[t : t + 1, :])
         dproj_n = dproj_n.astype(BF16)
-        dlin_n = dot_last(dproj_n, ns[t]) * slope_n[t]
+        dlin_n = dot_last(dproj_n, ns_c[t]) * slope_n[t]
         dbias_n = jnp.sum(dlin_n, axis=0, keepdims=True)
         dlin_n = dlin_n.astype(BF16)
         dsummed = dot_last(dlin_n, nf[t, 128:256, :]).astype(BF16)
@@ -322,7 +326,7 @@
 
         def node_grads():
             grads[node_at : node_at + 256, :] = dot_first(node_in[t], dlin_n).astype(BF16)
-            grads[node_at + 256 : node_at + 384, :] = dot_first(act_n[t], dproj_n).astype(BF16)
+            grads[node_at + 256 : node_at + 384, :] = centred(dot_first(act_n[t], dproj_n)).astype(BF16)
 
         small_rows = 128 if last else units[NODE0]
         if not last:
@@ -341,7 +345,7 @@
             dgain_e = dgain_e + dg
             dp = dp.astype(BF16)
             dproj[at, :] = dp
-            dl = (dot_last(dp, es[t]) * slope_e[t, at, :]).astype(BF16)
+            dl = (dot_last(dp, es_c[t]) * slope_e[t, at, :]).astype(BF16)
             dlin[at, :] = dl
             dold = dnew + dot_last(dl, ef[t, 256:384, :])
             if last:
@@ -366,7 +370,7 @@
         grads[edge_at + 128 : edge_at + 256, :] = dot_first(h, sums_b[384:640]).astype(BF16)
         old = edges[...] if t == 0 else rest[:, 128:256]
         grads[edge_at + 256 : edge_at + 384, :] = dot_first(old, dlin[...]).astype(BF16)
-        grads[edge_at + 384 : edge_at + 512, :] = dot_first(act_e[t], dproj[...]).astype(BF16)
+        grads[edge_at + 384 : edge_at + 512, :] = centred(dot_first(act_e[t], dproj[...])).astype(BF16)
         grads[small_at : small_at + small_rows, :] = jnp.concatenate(
             [dbias_e, dgain_e, dbias_n, dgain_n, jnp.zeros((small_rows - 4, D), F32)], axis=0
         ).astype(BF16)
@@ -479,6 +483,8 @@
             pltpu.VMEM((SLOTS, D), BF16),
             pltpu.VMEM((SLOTS, D), BF16),
             pltpu.VMEM((NODES, D), F32),
+            pltpu.VMEM((STEPS, D, D), BF16),
+            pltpu.VMEM((STEPS, D, D), BF16),
             pltpu.VMEM((2 * STEPS, 4 * HALO, D), BF16),
             pltpu.VMEM((2 * STEPS, 4 * HALO, D), BF16),
             pltpu.VMEM((sum(ROWS), D), BF16),

time: 57.1 us -> 56.4 us (0.988)
  Pallas kernels: 55.7 us -> 54.9 us
    pallas_call x1, Pallas kernels: 54.5 us -> 53.8 us  [per_device(): pl.pallas_call(kernel, out_shape=(jax.ShapeDtypeStruct((NODES, D), BF16),...]
where the time goes in v5:
time: 56.4 us; the launch traced here: 56.2 us
  Pallas kernels  54.9 us (97%)
  between operations  1.3 us (2%)
    pallas_call x1, Pallas kernels, per_device(): pl.pallas_call(kernel, out_shape=(jax.ShapeDtypeStruct((NODES, D), BF16),...  53.8 us

profile of v5, /device:TPU:1, one launch (start us, length us, event | category | flops | bytes accessed | tf_op | source)
XLA Modules:
  0.0 56.2 jit_solution(5492986157488444336)
XLA Ops:
  1.3 53.8 %steps.1 = (bf16[256,128]{1,0:T(8,128)(2,1)S(1)}, bf16[1024,128]{1,0:T(8,128)(2,1)S(1)}, bf16[2048,128]{1,0:T(8,128)(2,1)S(1)}) custom-call(bf16[256,128]{1,0:T(8,128)(2,1)} %refs_0_.1, bf16[1024,128]{1,0:T(8,128)(2,1)} %refs_1_.1, s32[8,128]{1,0:T(8,128)} %bitcast.2, s32[8,128]{1,0:T(8,128)} %bitcast.3, s32[1,4,32]{2,1,0:T(4,128)} %refs_4_.1, ...), custom_call_target="tpu_custom_call" | custom-call | tf_op jit(solution)/shard_map/steps/pallas_call | solution.py:455
  55.1 1.1 %finish.1 = (bf16[256,128]{1,0:T(8,128)(2,1)}, bf16[1024,128]{1,0:T(8,128)(2,1)}, f32[2,384,128]{2,1,0:T(8,128)}, f32[2,128]{1,0:T(2,128)}, f32[2,128,128]{2,1,0...) custom-call(bf16[256,128]{1,0:T(8,128)(2,1)S(1)} %get-tuple-element., ...), custom_call_target="tpu_custom_call" | custom-call | tf_op jit(solution)/shard_map/finish/pallas_call | solution.py:506

commit v6 on v5

--- a/solution.py
+++ b/solution.py
@@ -13,7 +13,7 @@
 EPS = 1e-05
 YH, YL, ZH, C, X, ZL = 4, 2, 4, 2, 4, 2
 NODES, SLOTS, D, HALO = 256, 1024, 128, 32
-CHUNK = 512
+CHUNK, BACK_CHUNK = 512, 1024
 STEP1, NODE0, EDGE0 = 0, 1, 2
 ROWS = (1024, 512, 512)
 BASE = (0, 1024, 1536)
@@ -67,7 +67,7 @@
     (
     own_pick, rest, spread, hal_pad, h1, part, act_e, slope_e, xhat_e, inv_e, act_n, slope_n, xhat_n, inv_n,
     node_in, edge_new, de, dlin, dproj, dh,
-    es_c, ns_c, halo_out, halo_in, grads, mid, got1_a, got1_b, got1_c, got2_a, got2_b, got2_c,
+    edges_t, act_t, es_c, ns_c, halo_out, halo_in, grads, mid, got1_a, got1_b, got1_c, got2_a, got2_b, got2_c,
     in_sem, halo_ssem, halo_rsem, red_ssem, red_rsem, ready,
     ) = refs
     sector, span = lax.axis_index("sector"), lax.axis_index("span")
@@ -139,6 +139,8 @@
     outside = ((row_id >= 2 * HALO) & (row_id < 3 * HALO) & (span == 0)) | (
         (row_id >= 3 * HALO) & (span == n_span - 1)
     )
+
+    apart = pl.when(sector >= 0)
 
     def exchange_start(t):
         for k in range(4):
@@ -185,19 +187,26 @@
     for i in rest_loads:
         loads[i].wait()
 
+    edges_t[...] = edges[...].T
     for t in range(STEPS):
         es_c[t] = centred(es[t]).astype(BF16)
         ns_c[t] = centred(ns[t]).astype(BF16)
 
     def forward(t):
         h = nodes[...] if t == 0 else h1[...]
-        own_table = jnp.concatenate(
-            [dot(h, ef[t, 0:128, :]).astype(BF16), dot(h, ef[t, 128:256, :]).astype(BF16)], axis=0
-        )
         bias, gain = eb[t : t + 1, :], eg[t : t + 1, :]
-        for i in range(SLOTS // CHUNK):
-            at = pl.ds(i * CHUNK, CHUNK)
-            part[at, :] = dot(own_pick[at, :], own_table) + bias
+
+        @apart
+        def _():
+            own_table = jnp.concatenate(
+                [dot(h, ef[t, 0:128, :]).astype(BF16), dot(h, ef[t, 128:256, :]).astype(BF16)], axis=0
+            )
+            for i in range(SLOTS // CHUNK):
+                at = pl.ds(i * CHUNK, CHUNK)
+                part[at, :] = dot(own_pick[at, :], own_table) + bias
+            if t == 1:
+                act_t[...] = act_e[0].T
+
         exchange_wait(t)
         halo_in[t] = jnp.where(outside, 0.0, halo_in[t].astype(F32)).astype(BF16)
         rest_table = jnp.concatenate(
@@ -336,63 +345,88 @@
             reduce_start(NODE0, held=held)
         dgain_e = jnp.zeros((1, D), F32)
         gain = eg[t : t + 1, :]
-        for i in range(SLOTS // CHUNK):
-            at = pl.ds(i * CHUNK, CHUNK)
+        for i in range(SLOTS // BACK_CHUNK):
+            at = pl.ds(i * BACK_CHUNK, BACK_CHUNK)
             dnew = dot(own_pick[at, 256:512], dsummed)
             if not last:
                 dnew = dnew + de[at, :]
+            de[at, :] = dnew
             dp, dg = normalized_back(dnew, xhat_e[t, at, :], inv_e[t, at, :], gain)
             dgain_e = dgain_e + dg
             dp = dp.astype(BF16)
             dproj[at, :] = dp
             dl = (dot_last(dp, es_c[t]) * slope_e[t, at, :]).astype(BF16)
             dlin[at, :] = dl
-            dold = dnew + dot_last(dl, ef[t, 256:384, :])
-            if last:
-                de[at, :] = dold
-            else:
-                edge_grad[at, :] = dold.astype(BF16)
-        sums = dot(spread[...], dlin[...])
-        sums_b = sums.astype(BF16)
-        dbias_e = jnp.sum(sums[384:640], axis=0, keepdims=True)
-
-        def send_back():
-            dhalo = dot_last(sums_b[256:384], ef[t, 0:128, :])
+
+        def send_back(sums):
+            dhalo = dot_last(sums.astype(BF16), ef[t, 0:128, :])
             halo_out[STEPS + t] = jnp.where(outside, 0.0, dhalo).astype(BF16)
             exchange_start(STEPS + t)
 
         edge_at = BASE[STEP1] if last else BASE[EDGE0]
+
+        def edge_grads(sums, sums_b):
+            grads[edge_at : edge_at + 128, :] = (
+                dot_first(h, sums_b[0:256]) + dot_first(halo_in[t], sums_b[256:384])
+            ).astype(BF16)
+            grads[edge_at + 128 : edge_at + 256, :] = dot_first(h, sums_b[384:640]).astype(BF16)
+            grads[edge_at + 256 : edge_at + 384, :] = (dot_first(rest[:, 128:256], dlin[...]) if last else dot(edges_t[...], dlin[...])).astype(BF16)
+            grads[edge_at + 384 : edge_at + 512, :] = centred(
+                dot_first(act_e[t], dproj[...]) if last else dot(act_t[...], dproj[...])
+            ).astype(BF16)
+            dbias_e = jnp.sum(sums[384:640], axis=0, keepdims=True)
+            grads[small_at : small_at + small_rows, :] = jnp.concatenate(
+                [dbias_e, dgain_e, dbias_n, dgain_n, jnp.zeros((small_rows - 4, D), F32)], axis=0
+            ).astype(BF16)
+
+        def own_part(sums_b):
+            dh[...] = (
+                dy
+                + dot_last(dlin_n, nf[t, 0:128, :])
+                + dot_last(sums_b[0:256], ef[t, 0:128, :])
+                + dot_last(sums_b[384:640], ef[t, 128:256, :])
+            )
+
+        def older_edges():
+            for i in range(SLOTS // BACK_CHUNK):
+                at = pl.ds(i * BACK_CHUNK, BACK_CHUNK)
+                dold = de[at, :] + dot_last(dlin[at, :], ef[t, 256:384, :])
+                if last:
+                    de[at, :] = dold
+                else:
+                    edge_grad[at, :] = dold.astype(BF16)
+
         if last:
-            send_back()
-        grads[edge_at : edge_at + 128, :] = (
-            dot_first(h, sums_b[0:256]) + dot_first(halo_in[t], sums_b[256:384])
-        ).astype(BF16)
-        grads[edge_at + 128 : edge_at + 256, :] = dot_first(h, sums_b[384:640]).astype(BF16)
-        old = edges[...] if t == 0 else rest[:, 128:256]
-        grads[edge_at + 256 : edge_at + 384, :] = dot_first(old, dlin[...]).astype(BF16)
-        grads[edge_at + 384 : edge_at + 512, :] = centred(dot_first(act_e[t], dproj[...])).astype(BF16)
-        grads[small_at : small_at + small_rows, :] = jnp.concatenate(
-            [dbias_e, dgain_e, dbias_n, dgain_n, jnp.zeros((small_rows - 4, D), F32)], axis=0
-        ).astype(BF16)
-        if last:
-            node_grads()
-            reduce_start(STEP1)
+            send_back(dot(spread[256:384, :], dlin[...]))
+
+            @apart
+            def _():
+                sums = dot(spread[...], dlin[...])
+                sums_b = sums.astype(BF16)
+                edge_grads(sums, sums_b)
+                node_grads()
+                reduce_start(STEP1)
+                own_part(sums_b)
+                older_edges()
         else:
+            sums = dot(spread[...], dlin[...])
+            sums_b = sums.astype(BF16)
+            edge_grads(sums, sums_b)
             reduce_start(EDGE0)
             reduce_start(NODE0, only=held)
-            send_back()
-        own = (
-            dy
-            + dot_last(dlin_n, nf[t, 0:128, :])
-            + dot_last(sums_b[0:256], ef[t, 0:128, :])
-            + dot_last(sums_b[384:640], ef[t, 128:256, :])
-        )
+
+            @apart
+            def _():
+                send_back(sums[256:384])
+                own_part(sums_b)
+                older_edges()
+
         if not last:
             pl.semaphore_wait(ready, YH - 1)
             reduce_middle(STEP1)
             reduce_middle(NODE0)
         exchange_wait(STEPS + t)
-        own = (own + dot(halo_spread, halo_in[STEPS + t])).astype(BF16)
+        own = (dh[...] + dot(halo_spread, halo_in[STEPS + t])).astype(BF16)
         if last:
             dh[...] = own.astype(F32)
         else:
@@ -483,6 +517,8 @@
             pltpu.VMEM((SLOTS, D), BF16),
             pltpu.VMEM((SLOTS, D), BF16),
             pltpu.VMEM((NODES, D), F32),
+            pltpu.VMEM((D, SLOTS), BF16),
+            pltpu.VMEM((D, SLOTS), BF16),
             pltpu.VMEM((STEPS, D, D), BF16),
             pltpu.VMEM((STEPS, D, D), BF16),
             pltpu.VMEM((2 * STEPS, 4 * HALO, D), BF16),

time: 56.4 us -> 55.8 us (0.989)
  no operation moved by 1% of the time
where the time goes in v6:
time: 55.8 us; the launch traced here: 55.7 us
  Pallas kernels  54.4 us (97%)
  between operations  1.3 us (2%)
    pallas_call x1, Pallas kernels, per_device(): pl.pallas_call(kernel, out_shape=(jax.ShapeDtypeStruct((NODES, D), BF16),...  53.2 us
    pallas_call x1, Pallas kernels, per_device(): pl.pallas_call(finish, out_shape=(jax.ShapeDtypeStruct((NODES, D), BF16),...  1.12 us

profile of v6, /device:TPU:1, one launch (start us, length us, event | category | flops | bytes accessed | tf_op | source)
XLA Modules:
  0.0 55.7 jit_solution(14682859111112852150)
XLA Ops:
  1.3 53.2 %steps.1 = (bf16[256,128]{1,0:T(8,128)(2,1)S(1)}, bf16[1024,128]{1,0:T(8,128)(2,1)S(1)}, bf16[2048,128]{1,0:T(8,128)(2,1)S(1)}) custom-call(bf16[256,128]{1,0:T(8,128)(2,1)} %refs_0_.1, bf16[1024,128]{1,0:T(8,128)(2,1)} %refs_1_.1, s32[8,128]{1,0:T(8,128)} %bitcast.2, s32[8,128]{1,0:T(8,128)} %bitcast.3, s32[1,4,32]{2,1,0:T(4,128)} %refs_4_.1, ...), custom_call_target="tpu_custom_call" | custom-call | tf_op jit(solution)/shard_map/steps/pallas_call | solution.py:489
  54.5 1.1 %finish.1 = (bf16[256,128]{1,0:T(8,128)(2,1)}, bf16[1024,128]{1,0:T(8,128)(2,1)}, f32[2,384,128]{2,1,0:T(8,128)}, f32[2,128]{1,0:T(2,128)}, f32[2,128,128]{2,1,0...) custom-call(bf16[256,128]{1,0:T(8,128)(2,1)S(1)} %get-tuple-element., ...), custom_call_target="tpu_custom_call" | custom-call | tf_op jit(solution)/shard_map/finish/pallas_call | solution.py:542

commit v7 on v6

--- a/solution.py
+++ b/solution.py
@@ -18,6 +18,7 @@
 ROWS = (1024, 512, 512)
 BASE = (0, 1024, 1536)
 SMALL = (896, 384)
+JOINED = ((STEP1,), (NODE0, EDGE0))
 
 
 def dot(a, b):
@@ -67,7 +68,7 @@
     (
     own_pick, rest, spread, hal_pad, h1, part, act_e, slope_e, xhat_e, inv_e, act_n, slope_n, xhat_n, inv_n,
     node_in, edge_new, de, dlin, dproj, dh,
-    edges_t, act_t, es_c, ns_c, halo_out, halo_in, grads, mid, got1_a, got1_b, got1_c, got2_a, got2_b, got2_c,
+    edges_t, act_t, es_c, ns_c, halo_out, halo_in, grads, mid, got1_a, got1_b, got1_c, got2_a, got2_b,
     in_sem, halo_ssem, halo_rsem, red_ssem, red_rsem, ready,
     ) = refs
     sector, span = lax.axis_index("sector"), lax.axis_index("span")
@@ -78,7 +79,9 @@
     g1, g2 = YL * ZL * X * C, YH * ZH
     me1, me2 = ((yl * ZL + zl) * X + x) * C + c, yh * ZH + zh
     units = tuple(n // g1 for n in ROWS)
-    got1, got2 = (got1_a, got1_b, got1_c), (got2_a, got2_b, got2_c)
+    got1, got2 = (got1_a, got1_b, got1_c), (got2_a, got2_b)
+    wide = tuple(sum(units[i] for i in members) for members in JOINED)
+    wide_base = tuple(BASE[members[0]] for members in JOINED)
 
     def turned(at, size):
         return [at] + [lax.rem(at + k, size) for k in range(1, size)]
@@ -266,58 +269,60 @@
             else:
                 pl.when(j != held)(functools.partial(copy, j, peer))
 
-    def reduce_middle(i):
-        unit = units[i]
-        others = got1[i].at[pl.ds(1, g1 - 1)]
-        pltpu.make_async_copy(others, others, red_rsem.at[i, 0]).wait()
-        got1[i][me1] = grads[pl.ds(pl.multiple_of(BASE[i] + me1 * unit, unit), unit), :]
-        acc = got1[i][0].astype(F32)
-        for k in range(1, g1):
-            acc = acc + got1[i][k].astype(F32)
-        acc = acc.astype(BF16)
-        block = pl.ds(BASE[i] // g1, unit)
-        mid[block, :] = acc
-        got2[i][me2] = acc
-
+    def reduce_middle(w):
+        for i in JOINED[w]:
+            unit = units[i]
+            others = got1[i].at[pl.ds(1, g1 - 1)]
+            pltpu.make_async_copy(others, others, red_rsem.at[i, 0]).wait()
+            got1[i][me1] = grads[pl.ds(pl.multiple_of(BASE[i] + me1 * unit, unit), unit), :]
+            acc = got1[i][0].astype(F32)
+            for k in range(1, g1):
+                acc = acc + got1[i][k].astype(F32)
+            mid[pl.ds(BASE[i] // g1, unit), :] = acc.astype(BF16)
+        block = pl.ds(wide_base[w] // g1, wide[w])
+        got2[w][me2] = mid[block, :]
         for peer in peers2:
             pltpu.make_async_remote_copy(
                 src_ref=mid.at[block],
-                dst_ref=got2[i].at[me2],
-                send_sem=red_ssem.at[i, 1],
-                recv_sem=red_rsem.at[i, 1],
+                dst_ref=got2[w].at[me2],
+                send_sem=red_ssem.at[w, 1],
+                recv_sem=red_rsem.at[w, 1],
                 device_id=peer,
                 device_id_type=MESH,
             ).start()
 
-    def reduce_last(i):
-        unit = units[i]
-        others = got2[i].at[pl.ds(1, g2 - 1)]
-        pltpu.make_async_copy(others, others, red_rsem.at[i, 1]).wait()
-        acc = got2[i][0].astype(F32)
+    def reduce_last(w):
+        others = got2[w].at[pl.ds(1, g2 - 1)]
+        pltpu.make_async_copy(others, others, red_rsem.at[w, 1]).wait()
+        acc = got2[w][0].astype(F32)
         for k in range(1, g2):
-            acc = acc + got2[i][k].astype(F32)
+            acc = acc + got2[w][k].astype(F32)
         scale = jnp.float32(NODES * n_sector * n_span) ** (-0.5)
-        mine = pl.ds(pl.multiple_of(BASE[i] + me1 * unit, unit), unit)
+        mine = pl.ds(pl.multiple_of(wide_base[w] + me1 * wide[w], wide[w]), wide[w])
         total[mine, :] = (acc * scale).astype(BF16)
-
         for _, peer in peers1:
             pltpu.make_async_remote_copy(
                 src_ref=total.at[mine],
                 dst_ref=total.at[mine],
-                send_sem=red_ssem.at[i, 2],
-                recv_sem=red_rsem.at[i, 2],
+                send_sem=red_ssem.at[w, 2],
+                recv_sem=red_rsem.at[w, 2],
                 device_id=peer,
                 device_id_type=MESH,
             ).start()
 
-    def reduce_finish(i):
-        others = total.at[pl.ds(BASE[i], ROWS[i] - units[i])]
-        pltpu.make_async_copy(others, others, red_rsem.at[i, 2]).wait()
-
-    def reduce_sent(i):
-        for phase, ref, count in ((0, got1[i], g1), (1, got2[i], g2), (2, got1[i], g1)):
-            sent = ref.at[pl.ds(1, count - 1)]
-            pltpu.make_async_copy(sent, sent, red_ssem.at[i, phase]).wait()
+    def reduce_finish(w):
+        others = total.at[pl.ds(wide_base[w], (g1 - 1) * wide[w])]
+        pltpu.make_async_copy(others, others, red_rsem.at[w, 2]).wait()
+
+    def reduce_sent():
+        for i in (STEP1, NODE0, EDGE0):
+            sent = got1[i].at[pl.ds(1, g1 - 1)]
+            pltpu.make_async_copy(sent, sent, red_ssem.at[i, 0]).wait()
+        for w in range(2):
+            sent = got2[w].at[pl.ds(1, g2 - 1)]
+            pltpu.make_async_copy(sent, sent, red_ssem.at[w, 1]).wait()
+            sent = total.at[pl.ds(wide_base[w], (g1 - 1) * wide[w])]
+            pltpu.make_async_copy(sent, sent, red_ssem.at[w, 2]).wait()
 
     def backward(t):
         last = t + 1 == STEPS
@@ -423,8 +428,8 @@
 
         if not last:
             pl.semaphore_wait(ready, YH - 1)
-            reduce_middle(STEP1)
-            reduce_middle(NODE0)
+            reduce_middle(0)
+            reduce_middle(1)
         exchange_wait(STEPS + t)
         own = (dh[...] + dot(halo_spread, halo_in[STEPS + t])).astype(BF16)
         if last:
@@ -436,13 +441,11 @@
     forward(1)
     backward(1)
     backward(0)
-    reduce_middle(EDGE0)
-    for i in (STEP1, NODE0, EDGE0):
-        reduce_last(i)
-    for i in (STEP1, NODE0, EDGE0):
-        reduce_finish(i)
-    for i in (STEP1, NODE0, EDGE0):
-        reduce_sent(i)
+    for w in range(2):
+        reduce_last(w)
+    for w in range(2):
+        reduce_finish(w)
+    reduce_sent()
     for t in range(2 * STEPS):
         pltpu.make_async_copy(halo_out.at[t], halo_out.at[t], halo_ssem.at[t]).wait()
 
@@ -452,18 +455,18 @@
     copies = [pltpu.make_async_copy(edge_grad, outs[1], sem.at[0]), pltpu.make_async_copy(node_grad, outs[0], sem.at[1])]
     for copy in copies:
         copy.start()
-    where = ((BASE[EDGE0], BASE[STEP1]), (BASE[NODE0], BASE[STEP1] + 512))
-    for out, part, first, count in ((2, 0, 0, 384), (4, 0, 384, 128), (6, 1, 0, 256), (8, 1, 256, 128)):
-        to = part * 512 + first
-        for t in range(STEPS):
-            start = where[part][t] + first
-            wide[t, to : to + count, :] = total[start : start + count, :].astype(F32)
-        copy = pltpu.make_async_copy(wide.at[:, pl.ds(to, count), :], outs[out], sem.at[out])
+    unit = ROWS[NODE0] // (YL * ZL * X * C)
+    joined = total[BASE[NODE0] :, :].astype(F32).reshape(-1, 2 * unit, D)
+    node0, edge0 = joined[:, :unit].reshape(ROWS[NODE0], D), joined[:, unit:].reshape(ROWS[EDGE0], D)
+    for out, step0, first, count, at in (
+        (2, edge0, 0, 384, 0), (4, edge0, 384, 128, 384), (6, node0, 0, 256, 512), (8, node0, 256, 128, 768)
+    ):
+        wide[0, at : at + count, :] = step0[first : first + count, :]
+        wide[1, at : at + count, :] = total[at : at + count, :].astype(F32)
+        copy = pltpu.make_async_copy(wide.at[:, pl.ds(at, count), :], outs[out], sem.at[out])
         copy.start()
         copies.append(copy)
-    smalls = (BASE[NODE0] + SMALL[NODE0], BASE[STEP1] + SMALL[STEP1])
-    for t in range(STEPS):
-        rows = total[smalls[t] : smalls[t] + 16, :].astype(F32)
+    for t, rows in enumerate((node0[384:400], total[SMALL[STEP1] : SMALL[STEP1] + 16, :].astype(F32))):
         for k in range(4):
             small[k, t : t + 1, :] = rows[k : k + 1, :]
     for k, out in enumerate((3, 5, 7, 9)):
@@ -526,7 +529,7 @@
             pltpu.VMEM((sum(ROWS), D), BF16),
             pltpu.VMEM((sum(ROWS) // g1, D), BF16),
             *(pltpu.VMEM((g1, n // g1, D), BF16) for n in ROWS),
-            *(pltpu.VMEM((g2, n // g1, D), BF16) for n in ROWS),
+            *(pltpu.VMEM((g2, sum(ROWS[i] for i in members) // g1, D), BF16) for members in JOINED),
             pltpu.SemaphoreType.DMA((14,)),
             pltpu.SemaphoreType.DMA((2 * STEPS,)),
             pltpu.SemaphoreType.DMA((2 * STEPS,)),

time: 55.8 us -> 55.4 us (level)
  no operation moved by 1% of the time
where the time goes in v7:
time: 55.4 us; the launch traced here: 55.2 us
  Pallas kernels  53.9 us (97%)
  between operations  1.3 us (2%)
    pallas_call x1, Pallas kernels, per_device(): pl.pallas_call(kernel, out_shape=(jax.ShapeDtypeStruct((NODES, D), BF16),...  52.8 us
    pallas_call x1, Pallas kernels, per_device(): pl.pallas_call(finish, out_shape=(jax.ShapeDtypeStruct((NODES, D), BF16),...  1.12 us

profile of v7, /device:TPU:1, one launch (start us, length us, event | category | flops | bytes accessed | tf_op | source)
XLA Modules:
  0.0 55.2 jit_solution(17813651078045791016)
XLA Ops:
  1.3 52.8 %steps.1 = (bf16[256,128]{1,0:T(8,128)(2,1)S(1)}, bf16[1024,128]{1,0:T(8,128)(2,1)S(1)}, bf16[2048,128]{1,0:T(8,128)(2,1)S(1)}) custom-call(bf16[256,128]{1,0:T(8,128)(2,1)} %refs_0_.1, bf16[1024,128]{1,0:T(8,128)(2,1)} %refs_1_.1, s32[8,128]{1,0:T(8,128)} %bitcast.2, s32[8,128]{1,0:T(8,128)} %bitcast.3, s32[1,4,32]{2,1,0:T(4,128)} %refs_4_.1, ...), custom_call_target="tpu_custom_call" | custom-call | tf_op jit(solution)/shard_map/steps/pallas_call | solution.py:492
  54.1 1.1 %finish.1 = (bf16[256,128]{1,0:T(8,128)(2,1)}, bf16[1024,128]{1,0:T(8,128)(2,1)}, f32[2,384,128]{2,1,0:T(8,128)}, f32[2,128]{1,0:T(2,128)}, f32[2,128,128]{2,1,0...) custom-call(bf16[256,128]{1,0:T(8,128)(2,1)S(1)} %get-tuple-element., ...), custom_call_target="tpu_custom_call" | custom-call | tf_op jit(solution)/shard_map/finish/pallas_call | solution.py:545

commit v8 on v7

--- a/solution.py
+++ b/solution.py
@@ -112,8 +112,23 @@
     for peer in around:
         pl.semaphore_signal(barrier, inc=1, device_id=peer, device_id_type=MESH)
 
-    lines = [peer for peer, (a, b) in zip(peers2, offsets2) if b == 0]
-    greeted = [peer for _, peer in peers1] + [peer for peer, (a, b) in zip(peers2, offsets2) if a == 0 or b == 0]
+    beside = [
+        peer
+        for peer, (a, b) in zip(peers2, offsets2)
+        if (b == 0 and a in (1, YH - 1)) or (a == 0 and b in (1, ZH - 1))
+    ]
+    greeted = beside + [
+        peer for (_, peer), o in zip(peers1, offsets1) if o[0] + o[1] + min(o[2], X - o[2]) <= 3
+    ]
+    beside = beside + [peer for (_, peer), o in zip(peers1, offsets1) if o[0] and o[1:] == (0, 0, 0)]
+
+    def tell(turn):
+        for peer in beside:
+            pl.semaphore_signal(ready.at[turn], inc=1, device_id=peer, device_id_type=MESH)
+
+    def hear(turn):
+        pl.semaphore_wait(ready.at[turn], len(beside))
+
     for peer in greeted:
         pl.semaphore_signal(barrier, inc=1, device_id=peer, device_id_type=MESH)
 
@@ -162,8 +177,7 @@
     halo_out[0] = dot(halo_pick, nodes[...]).astype(BF16)
     pl.semaphore_wait(barrier, 4 + len(greeted))
     exchange_start(0)
-    for peer in lines:
-        pl.semaphore_signal(ready, inc=1, device_id=peer, device_id_type=MESH)
+    tell(0)
 
     for i in first[2:]:
         loads[i].wait()
@@ -427,7 +441,7 @@
                 older_edges()
 
         if not last:
-            pl.semaphore_wait(ready, YH - 1)
+            hear(2)
             reduce_middle(0)
             reduce_middle(1)
         exchange_wait(STEPS + t)
@@ -438,7 +452,11 @@
             node_grad[...] = own
 
     forward(0)
+    hear(0)
+    tell(1)
     forward(1)
+    hear(1)
+    tell(2)
     backward(1)
     backward(0)
     for w in range(2):
@@ -535,7 +553,7 @@
             pltpu.SemaphoreType.DMA((2 * STEPS,)),
             pltpu.SemaphoreType.DMA((3, 3)),
             pltpu.SemaphoreType.DMA((3, 3)),
-            pltpu.SemaphoreType.REGULAR,
+            pltpu.SemaphoreType.REGULAR((3,)),
         ],
         compiler_params=pltpu.CompilerParams(
             collective_id=0, has_side_effects=True, vmem_limit_bytes=40 * 1024 * 1024

time: 55.4 us -> 54.8 us (0.989)
  no operation moved by 1% of the time
where the time goes in v8:
time: 54.8 us; the launch traced here: 54.7 us
  Pallas kernels  53.4 us (97%)
  between operations  1.3 us (2%)
    pallas_call x1, Pallas kernels, per_device(): pl.pallas_call(kernel, out_shape=(jax.ShapeDtypeStruct((NODES, D), BF16),...  52.3 us
    pallas_call x1, Pallas kernels, per_device(): pl.pallas_call(finish, out_shape=(jax.ShapeDtypeStruct((NODES, D), BF16),...  1.12 us

profile of v8, /device:TPU:1, one launch (start us, length us, event | category | flops | bytes accessed | tf_op | source)
XLA Modules:
  0.0 54.7 jit_solution(10781823863282422318)
XLA Ops:
  1.3 52.3 %steps.1 = (bf16[256,128]{1,0:T(8,128)(2,1)S(1)}, bf16[1024,128]{1,0:T(8,128)(2,1)S(1)}, bf16[2048,128]{1,0:T(8,128)(2,1)S(1)}) custom-call(bf16[256,128]{1,0:T(8,128)(2,1)} %refs_0_.1, bf16[1024,128]{1,0:T(8,128)(2,1)} %refs_1_.1, s32[8,128]{1,0:T(8,128)} %bitcast.2, s32[8,128]{1,0:T(8,128)} %bitcast.3, s32[1,4,32]{2,1,0:T(4,128)} %refs_4_.1, ...), custom_call_target="tpu_custom_call" | custom-call | tf_op jit(solution)/shard_map/steps/pallas_call | solution.py:510
  53.6 1.1 %finish.1 = (bf16[256,128]{1,0:T(8,128)(2,1)}, bf16[1024,128]{1,0:T(8,128)(2,1)}, f32[2,384,128]{2,1,0:T(8,128)}, f32[2,128]{1,0:T(2,128)}, f32[2,128,128]{2,1,0...) custom-call(bf16[256,128]{1,0:T(8,128)(2,1)S(1)} %get-tuple-element., ...), custom_call_target="tpu_custom_call" | custom-call | tf_op jit(solution)/shard_map/finish/pallas_call | solution.py:563
